TPU v7x, 1024 devices: a whole 8x8x8 slice. The times are simulated.
1024 devices in a mesh: blk: 64 (over z, x), sub: 16 (over y, core).
Axes of the slice: x: 8, y: 8, z: 8, core: 2. Of those that a mesh axis runs over, the one named last changes fastest.
Arguments:
- pressure: float32 [1024, 512, 128], P('blk', 'sub'), may hold values from -6 to 6
- source: float32 [1024, 512, 128], P('blk', 'sub'), may hold values from -6 to 6
- inv_density: float32 [1024, 512, 128], P('blk', 'sub'), may hold values from 0.05 to 1
Outputs:
- corrected: float32 [1024, 512, 128], P('blk', 'sub')
All inputs are finite; a program needn't handle non-finite values.
Results may differ from a plain program's by a relative error of at most 0.00002.
Values sent between devices are 32-bit elements; how exact they have to be, the bound alone decides.
A program may use at most 64 MiB of HBM per device.

v0:
```python
import jax
import jax.numpy as jnp
from jax import lax
from jax.sharding import PartitionSpec as P

PRE = 2
POST = 2
COARSE_SWEEPS = 6


WEIGHT = 0.8


def padded_2(block, sides, width):
    for axis, dim in sides:
        count = lax.axis_size(axis)
        forward = [(i, i + 1) for i in range(count - 1)]
        backward = [(target, source) for source, target in forward]
        low = lax.ppermute(
            lax.slice_in_dim(block, block.shape[dim] - width, None, axis=dim), axis, forward
        )
        high = lax.ppermute(lax.slice_in_dim(block, 0, width, axis=dim), axis, backward)
        block = jnp.concatenate([low, block, high], axis=dim)
    return block


def shift_down(value):
    return jnp.pad(value[:, :, :-1], ((0, 0), (0, 0), (1, 0)))


def shift_up(value):
    return jnp.pad(value[:, :, 1:], ((0, 0), (0, 0), (0, 1)))


def face_coefs(padded):
    center = padded[1:-1, 1:-1]
    return (
        0.5 * (center + padded[:-2, 1:-1]),
        0.5 * (center + padded[2:, 1:-1]),
        0.5 * (center + padded[1:-1, :-2]),
        0.5 * (center + padded[1:-1, 2:]),
        0.5 * (center + shift_down(center)),
        0.5 * (center + shift_up(center)),
    )


def apply_operator(padded, coefs, scale):
    center = padded[1:-1, 1:-1]
    total = coefs[0] * (center - padded[:-2, 1:-1]) + coefs[1] * (center - padded[2:, 1:-1])
    total = total + coefs[2] * (center - padded[1:-1, :-2]) + coefs[3] * (center - padded[1:-1, 2:])
    total = (
        total + coefs[4] * (center - shift_down(center)) + coefs[5] * (center - shift_up(center))
    )
    return scale * total


def inverse_diagonal(coefs, scale):
    total = coefs[0] + coefs[1] + coefs[2] + coefs[3] + coefs[4] + coefs[5]
    return WEIGHT / (scale * total)


def mean_yz(value):
    ext_x, ext_y, ext_z = value.shape
    return value.reshape(ext_x, ext_y // 2, 2, ext_z // 2, 2).mean(axis=(2, 4))


def mean_xz(value):
    ext_x, ext_y, ext_z = value.shape
    return value.reshape(ext_x // 2, 2, ext_y, ext_z // 2, 2).mean(axis=(1, 4))


def mean_xy(value):
    ext_x, ext_y, ext_z = value.shape
    return value.reshape(ext_x // 2, 2, ext_y // 2, 2, ext_z).mean(axis=(1, 3))


def coarsen_faces(coefs):
    return (
        mean_yz(coefs[0][0::2]),
        mean_yz(coefs[1][1::2]),
        mean_xz(coefs[2][:, 0::2]),
        mean_xz(coefs[3][:, 1::2]),
        mean_xy(coefs[4][:, :, 0::2]),
        mean_xy(coefs[5][:, :, 1::2]),
    )


def coarsen_cells(value):
    ext_x, ext_y, ext_z = value.shape
    return value.reshape(ext_x // 2, 2, ext_y // 2, 2, ext_z // 2, 2).mean(axis=(1, 3, 5))


def refine_cells(value):
    return jnp.repeat(jnp.repeat(jnp.repeat(value, 2, axis=0), 2, axis=1), 2, axis=2)


def widen_field(field):
    return padded_2(field, (("blk", 0), ("sub", 1)), 1)


def sweep(field, rhs_level, coefs, invd, scale):
    padded = widen_field(field)
    return field + invd * (rhs_level - apply_operator(padded, coefs, scale))


def residual(field, rhs_level, coefs, scale):
    padded = widen_field(field)
    return rhs_level - apply_operator(padded, coefs, scale)


def on_device(pressure, source, inv_density):
    padded_density = padded_2(inv_density, (("blk", 0), ("sub", 1)), 1)
    coefs0 = face_coefs(padded_density)
    invd0 = inverse_diagonal(coefs0, 1.0)

    def fine_pass(field):
        return sweep(field, source, coefs0, invd0, 1.0)

    pre_count = PRE
    post_count = POST
    coefs1 = coarsen_faces(coefs0)
    invd1 = inverse_diagonal(coefs1, 0.25)
    coefs2 = coarsen_faces(coefs1)
    field = pressure
    for sweep_index in range(pre_count):
        field = fine_pass(field)
    res0 = residual(field, source, coefs0, 1.0)
    rhs_one = coarsen_cells(res0)
    err_one = invd1 * rhs_one
    err_one = sweep(err_one, rhs_one, coefs1, invd1, 0.25)
    res1 = residual(err_one, rhs_one, coefs1, 0.25)
    level_post = POST
    rhs_two = coarsen_cells(res1)
    invd2 = inverse_diagonal(coefs2, 0.0625)
    err_two = invd2 * rhs_two
    for sweep_index in range(COARSE_SWEEPS):
        err_two = sweep(err_two, rhs_two, coefs2, invd2, 0.0625)
    err_one = err_one + refine_cells(err_two)
    for sweep_index in range(level_post):
        err_one = sweep(err_one, rhs_one, coefs1, invd1, 0.25)
    field = field + refine_cells(err_one)
    for sweep_index in range(post_count):
        field = fine_pass(field)
    return field


def solution(mesh):
    return jax.shard_map(
        on_device,
        mesh=mesh,
        in_specs=(P("blk", "sub", None), P("blk", "sub", None), P("blk", "sub", None)),
        out_specs=P("blk", "sub", None),
        check_vma=False,
    )
```

profile of v0, /device:TPU:447, one launch (start us, length us, event | category | flops | bytes accessed | tf_op | source)
XLA Modules:
  0.0 389.2 jit_solution(11528490950918345781)
XLA Ops:
  0.8 5.9 %collective-permute-start = (f32[1,32,128]{2,1,0:T(8,128)S(1)}, f32[1,32,128]{2,1,0:T(8,128)S(1)}, u32[]{:S(2)}, u32[]{:S(2)}) collective-permute-start(f32[1,32,128]{2,1,0:T(8,128)S(1)} %get-tuple-element.41), channel_id=1, source_target_pairs={{0,16},{16,32},{32,48},{48,64},{64,80},{80,96},{96,112},{112,128},... | collective-permute-start | bytes 49160 | tf_op jit(solution)/shard_map/ppermute | solution.py:19
  9.4 6.7 %collective-permute-start.4 = (f32[1,32,128]{2,1,0:T(8,128)S(1)}, f32[1,32,128]{2,1,0:T(8,128)S(1)}, u32[]{:S(2)}, u32[]{:S(2)}) collective-permute-start(f32[1,32,128]{2,1,0:T(8,128)S(1)} %get-tuple-element.47), channel_id=1, source_target_pairs={{0,16},{16,32},{32,48},{48,64},{64,80},{80,96},{96,112},{112,128},... | collective-permute-start | bytes 49160 | tf_op jit(solution)/shard_map/ppermute | solution.py:19
  19.1 5.9 %collective-permute-start.2 = (f32[18,1,128]{2,1,0:T(1,128)S(1)}, f32[18,1,128]{2,1,0:T(1,128)S(1)}, u32[]{:S(2)}, u32[]{:S(2)}) collective-permute-start(f32[18,1,128]{2,1,0:T(1,128)S(1)} %get-tuple-element.21), channel_id=1, source_target_pairs={{0,1},{1,2},{2,3},{3,4},{4,5},{5,6},{6,7},{7,8},{8,9},{9,10},{10,1... | collective-permute-start | bytes 27656 | tf_op jit(solution)/shard_map/ppermute | solution.py:19
  28.0 4.9 %collective-permute-start.6 = (f32[18,1,128]{2,1,0:T(1,128)S(1)}, f32[18,1,128]{2,1,0:T(1,128)S(1)}, u32[]{:S(2)}, u32[]{:S(2)}) collective-permute-start(f32[18,1,128]{2,1,0:T(1,128)S(1)} %get-tuple-element.22), channel_id=1, source_target_pairs={{0,1},{1,2},{2,3},{3,4},{4,5},{5,6},{6,7},{7,8},{8,9},{9,10},{10,1... | collective-permute-start | bytes 27656 | tf_op jit(solution)/shard_map/ppermute | solution.py:19
  39.6 7.0 %collective-permute-start.8 = (f32[1,32,128]{2,1,0:T(8,128)S(1)}, f32[1,32,128]{2,1,0:T(8,128)S(1)}, u32[]{:S(2)}, u32[]{:S(2)}) collective-permute-start(f32[1,32,128]{2,1,0:T(8,128)S(1)} %get-tuple-element.38), channel_id=1, source_target_pairs={{0,16},{16,32},{32,48},{48,64},{64,80},{80,96},{96,112},{112,128},... | collective-permute-start | bytes 49160 | tf_op jit(solution)/shard_map/ppermute | solution.py:19
  48.5 5.9 %collective-permute-done.9 = f32[1,32,128]{2,1,0:T(8,128)S(1)} collective-permute-done((f32[1,32,128]{2,1,0:T(8,128)S(1)}, f32[1,32,128]{2,1,0:T(8,128)S(1)}, u32[]{:S(2)}, u32[]{:S(2)}) %collective-permute-start.9) | collective-permute-done | bytes 16416 | tf_op jit(solution)/shard_map/ppermute | solution.py:22
  72.6 6.8 %slice.614 = f32[16,32,64]{2,1,0:T(8,128)} slice(f32[16,32,128]{2,1,0:T(8,128)S(1)} %get-tuple-element.6), slice={[0:16:1], [0:32:1], [0:128:2]} | slice | bytes 262144 | tf_op jit(solution)/shard_map/slice | solution.py:83
  79.4 6.9 %slice.615 = f32[16,32,64]{2,1,0:T(8,128)} slice(f32[16,32,128]{2,1,0:T(8,128)S(1)} %get-tuple-element.7), slice={[0:16:1], [0:32:1], [1:128:2]} | slice | bytes 262144 | tf_op jit(solution)/shard_map/slice | solution.py:84
  114.5 18.1 %reshape.66 = f32[8,2,16,2,64,2]{5,4,3,2,1,0:T(8,128)} reshape(f32[16,32,128]{2,1,0:T(8,128)S(1)} %fusion.37) | data formatting | bytes 524288 | tf_op jit(solution)/shard_map/reshape | solution.py:90
  132.5 7.0 %reduce_sum.132 = f32[8,16,64]{2,1,0:T(8,128)S(1)} reduce(f32[8,2,16,2,64,2]{5,4,3,2,1,0:T(8,128)} %reshape.66, f32[]{:T(128)} %constant.29.clone.1), dimensions={1,3,5}, to_apply=%region_6.7 | reduce | flops 57344 | bytes 294916 | tf_op jit(solution)/shard_map/reduce_sum | solution.py:90
  139.6 5.0 %collective-permute-start.16 = (f32[1,16,64]{2,1,0:T(8,128)S(1)}, f32[1,16,64]{2,1,0:T(8,128)S(1)}, u32[]{:S(2)}, u32[]{:S(2)}) collective-permute-start(f32[1,16,64]{2,1,0:T(8,128)S(1)} %get-tuple-element.77), channel_id=1, source_target_pairs={{0,16},{16,32},{32,48},{48,64},{64,80},{80,96},{96,112},{112,128},... | collective-permute-start | bytes 12296 | tf_op jit(solution)/shard_map/ppermute | solution.py:19
  146.5 5.8 %collective-permute-done.17 = f32[1,16,64]{2,1,0:T(8,128)S(1)} collective-permute-done((f32[1,16,64]{2,1,0:T(8,128)S(1)}, f32[1,16,64]{2,1,0:T(8,128)S(1)}, u32[]{:S(2)}, u32[]{:S(2)}) %collective-permute-start.17) | collective-permute-done | bytes 4128 | tf_op jit(solution)/shard_map/ppermute | solution.py:22
  157.7 4.1 %collective-permute-done.19 = f32[10,1,64]{2,1,0:T(1,128)S(1)} collective-permute-done((f32[10,1,64]{2,1,0:T(1,128)S(1)}, f32[10,1,64]{2,1,0:T(1,128)S(1)}, u32[]{:S(2)}, u32[]{:S(2)}) %collective-permute-start.19) | collective-permute-done | bytes 2592 | tf_op jit(solution)/shard_map/ppermute | solution.py:22
  179.3 4.1 %collective-permute-done.23 = f32[10,1,64]{2,1,0:T(1,128)S(1)} collective-permute-done((f32[10,1,64]{2,1,0:T(1,128)S(1)}, f32[10,1,64]{2,1,0:T(1,128)S(1)}, u32[]{:S(2)}, u32[]{:S(2)}) %collective-permute-start.23) | collective-permute-done | bytes 2592 | tf_op jit(solution)/shard_map/ppermute | solution.py:22
  188.3 5.0 %collective-permute-start.24 = (f32[1,8,32]{2,1,0:T(8,128)S(1)}, f32[1,8,32]{2,1,0:T(8,128)S(1)}, u32[]{:S(2)}, u32[]{:S(2)}) collective-permute-start(f32[1,8,32]{2,1,0:T(8,128)S(1)} %get-tuple-element.113), channel_id=1, source_target_pairs={{0,16},{16,32},{32,48},{48,64},{64,80},{80,96},{96,112},{112,128},... | collective-permute-start | bytes 3080 | tf_op jit(solution)/shard_map/ppermute | solution.py:19
  195.2 5.7 %collective-permute-done.25 = f32[1,8,32]{2,1,0:T(8,128)S(1)} collective-permute-done((f32[1,8,32]{2,1,0:T(8,128)S(1)}, f32[1,8,32]{2,1,0:T(8,128)S(1)}, u32[]{:S(2)}, u32[]{:S(2)}) %collective-permute-start.25) | collective-permute-done | bytes 1056 | tf_op jit(solution)/shard_map/ppermute | solution.py:22
  206.4 4.1 %collective-permute-done.27 = f32[6,1,32]{2,1,0:T(1,128)S(1)} collective-permute-done((f32[6,1,32]{2,1,0:T(1,128)S(1)}, f32[6,1,32]{2,1,0:T(1,128)S(1)}, u32[]{:S(2)}, u32[]{:S(2)}) %collective-permute-start.27) | collective-permute-done | bytes 800 | tf_op jit(solution)/shard_map/ppermute | solution.py:22
  216.7 4.3 %collective-permute-done.29 = f32[1,8,32]{2,1,0:T(8,128)S(1)} collective-permute-done((f32[1,8,32]{2,1,0:T(8,128)S(1)}, f32[1,8,32]{2,1,0:T(8,128)S(1)}, u32[]{:S(2)}, u32[]{:S(2)}) %collective-permute-start.29) | collective-permute-done | bytes 1056 | tf_op jit(solution)/shard_map/ppermute | solution.py:22
  226.1 4.1 %collective-permute-done.31 = f32[6,1,32]{2,1,0:T(1,128)S(1)} collective-permute-done((f32[6,1,32]{2,1,0:T(1,128)S(1)}, f32[6,1,32]{2,1,0:T(1,128)S(1)}, u32[]{:S(2)}, u32[]{:S(2)}) %collective-permute-start.31) | collective-permute-done | bytes 800 | tf_op jit(solution)/shard_map/ppermute | solution.py:22
  236.4 4.3 %collective-permute-done.33 = f32[1,8,32]{2,1,0:T(8,128)S(1)} collective-permute-done((f32[1,8,32]{2,1,0:T(8,128)S(1)}, f32[1,8,32]{2,1,0:T(8,128)S(1)}, u32[]{:S(2)}, u32[]{:S(2)}) %collective-permute-start.33) | collective-permute-done | bytes 1056 | tf_op jit(solution)/shard_map/ppermute | solution.py:22
  245.9 4.1 %collective-permute-done.35 = f32[6,1,32]{2,1,0:T(1,128)S(1)} collective-permute-done((f32[6,1,32]{2,1,0:T(1,128)S(1)}, f32[6,1,32]{2,1,0:T(1,128)S(1)}, u32[]{:S(2)}, u32[]{:S(2)}) %collective-permute-start.35) | collective-permute-done | bytes 800 | tf_op jit(solution)/shard_map/ppermute | solution.py:22
  256.2 4.3 %collective-permute-done.37 = f32[1,8,32]{2,1,0:T(8,128)S(1)} collective-permute-done((f32[1,8,32]{2,1,0:T(8,128)S(1)}, f32[1,8,32]{2,1,0:T(8,128)S(1)}, u32[]{:S(2)}, u32[]{:S(2)}) %collective-permute-start.37) | collective-permute-done | bytes 1056 | tf_op jit(solution)/shard_map/ppermute | solution.py:22
  265.6 4.1 %collective-permute-done.39 = f32[6,1,32]{2,1,0:T(1,128)S(1)} collective-permute-done((f32[6,1,32]{2,1,0:T(1,128)S(1)}, f32[6,1,32]{2,1,0:T(1,128)S(1)}, u32[]{:S(2)}, u32[]{:S(2)}) %collective-permute-start.39) | collective-permute-done | bytes 800 | tf_op jit(solution)/shard_map/ppermute | solution.py:22
  275.9 4.3 %collective-permute-done.41 = f32[1,8,32]{2,1,0:T(8,128)S(1)} collective-permute-done((f32[1,8,32]{2,1,0:T(8,128)S(1)}, f32[1,8,32]{2,1,0:T(8,128)S(1)}, u32[]{:S(2)}, u32[]{:S(2)}) %collective-permute-start.41) | collective-permute-done | bytes 1056 | tf_op jit(solution)/shard_map/ppermute | solution.py:22
  285.3 4.1 %collective-permute-done.43 = f32[6,1,32]{2,1,0:T(1,128)S(1)} collective-permute-done((f32[6,1,32]{2,1,0:T(1,128)S(1)}, f32[6,1,32]{2,1,0:T(1,128)S(1)}, u32[]{:S(2)}, u32[]{:S(2)}) %collective-permute-start.43) | collective-permute-done | bytes 800 | tf_op jit(solution)/shard_map/ppermute | solution.py:22
  295.7 4.3 %collective-permute-done.45 = f32[1,8,32]{2,1,0:T(8,128)S(1)} collective-permute-done((f32[1,8,32]{2,1,0:T(8,128)S(1)}, f32[1,8,32]{2,1,0:T(8,128)S(1)}, u32[]{:S(2)}, u32[]{:S(2)}) %collective-permute-start.45) | collective-permute-done | bytes 1056 | tf_op jit(solution)/shard_map/ppermute | solution.py:22
  305.1 4.1 %collective-permute-done.47 = f32[6,1,32]{2,1,0:T(1,128)S(1)} collective-permute-done((f32[6,1,32]{2,1,0:T(1,128)S(1)}, f32[6,1,32]{2,1,0:T(1,128)S(1)}, u32[]{:S(2)}, u32[]{:S(2)}) %collective-permute-start.47) | collective-permute-done | bytes 800 | tf_op jit(solution)/shard_map/ppermute | solution.py:22
  315.8 4.3 %collective-permute-done.49 = f32[1,16,64]{2,1,0:T(8,128)S(1)} collective-permute-done((f32[1,16,64]{2,1,0:T(8,128)S(1)}, f32[1,16,64]{2,1,0:T(8,128)S(1)}, u32[]{:S(2)}, u32[]{:S(2)}) %collective-permute-start.49) | collective-permute-done | bytes 4128 | tf_op jit(solution)/shard_map/ppermute | solution.py:22
  325.2 4.1 %collective-permute-done.51 = f32[10,1,64]{2,1,0:T(1,128)S(1)} collective-permute-done((f32[10,1,64]{2,1,0:T(1,128)S(1)}, f32[10,1,64]{2,1,0:T(1,128)S(1)}, u32[]{:S(2)}, u32[]{:S(2)}) %collective-permute-start.51) | collective-permute-done | bytes 2592 | tf_op jit(solution)/shard_map/ppermute | solution.py:22
  334.9 4.3 %collective-permute-done.53 = f32[1,16,64]{2,1,0:T(8,128)S(1)} collective-permute-done((f32[1,16,64]{2,1,0:T(8,128)S(1)}, f32[1,16,64]{2,1,0:T(8,128)S(1)}, u32[]{:S(2)}, u32[]{:S(2)}) %collective-permute-start.53) | collective-permute-done | bytes 4128 | tf_op jit(solution)/shard_map/ppermute | solution.py:22
  354.9 4.4 %collective-permute-done.57 = f32[1,32,128]{2,1,0:T(8,128)S(1)} collective-permute-done((f32[1,32,128]{2,1,0:T(8,128)S(1)}, f32[1,32,128]{2,1,0:T(8,128)S(1)}, u32[]{:S(2)}, u32[]{:S(2)}) %collective-permute-start.57) | collective-permute-done | bytes 16416 | tf_op jit(solution)/shard_map/ppermute | solution.py:22
  374.4 4.4 %collective-permute-done.61 = f32[1,32,128]{2,1,0:T(8,128)S(1)} collective-permute-done((f32[1,32,128]{2,1,0:T(8,128)S(1)}, f32[1,32,128]{2,1,0:T(8,128)S(1)}, u32[]{:S(2)}, u32[]{:S(2)}) %collective-permute-start.61) | collective-permute-done | bytes 16416 | tf_op jit(solution)/shard_map/ppermute | solution.py:22
  (272 shorter events, 215.2 us)
Async XLA Ops:
  0.8 17.2 %collective-permute-start = (f32[1,32,128]{2,1,0:T(8,128)S(1)}, f32[1,32,128]{2,1,0:T(8,128)S(1)}, u32[]{:S(2)}, u32[]{:S(2)}) collective-permute-start(f32[1,32,128]{2,1,0:T(8,128)S(1)} %get-tuple-element.41), channel_id=1, source_target_pairs={{0,16},{16,32},{32,48},{48,64},{64,80},{80,96},{96,112},{112,128},... | collective-permute-start | bytes 49160 | tf_op jit(solution)/shard_map/ppermute | solution.py:19
  6.7 12.3 %collective-permute-start.1 = (f32[1,32,128]{2,1,0:T(8,128)S(1)}, f32[1,32,128]{2,1,0:T(8,128)S(1)}, u32[]{:S(2)}, u32[]{:S(2)}) collective-permute-start(f32[1,32,128]{2,1,0:T(8,128)S(1)} %get-tuple-element.40), channel_id=1, source_target_pairs={{16,0},{32,16},{48,32},{64,48},{80,64},{96,80},{112,96},{128,112},... | collective-permute-start | bytes 49160 | tf_op jit(solution)/shard_map/ppermute | solution.py:22
  9.4 17.5 %collective-permute-start.4 = (f32[1,32,128]{2,1,0:T(8,128)S(1)}, f32[1,32,128]{2,1,0:T(8,128)S(1)}, u32[]{:S(2)}, u32[]{:S(2)}) collective-permute-start(f32[1,32,128]{2,1,0:T(8,128)S(1)} %get-tuple-element.47), channel_id=1, source_target_pairs={{0,16},{16,32},{32,48},{48,64},{64,80},{80,96},{96,112},{112,128},... | collective-permute-start | bytes 49160 | tf_op jit(solution)/shard_map/ppermute | solution.py:19
  16.1 11.8 %collective-permute-start.5 = (f32[1,32,128]{2,1,0:T(8,128)S(1)}, f32[1,32,128]{2,1,0:T(8,128)S(1)}, u32[]{:S(2)}, u32[]{:S(2)}) collective-permute-start(f32[1,32,128]{2,1,0:T(8,128)S(1)} %get-tuple-element.46), channel_id=1, source_target_pairs={{16,0},{32,16},{48,32},{64,48},{80,64},{96,80},{112,96},{128,112},... | collective-permute-start | bytes 49160 | tf_op jit(solution)/shard_map/ppermute | solution.py:22
  19.1 17.1 %collective-permute-start.2 = (f32[18,1,128]{2,1,0:T(1,128)S(1)}, f32[18,1,128]{2,1,0:T(1,128)S(1)}, u32[]{:S(2)}, u32[]{:S(2)}) collective-permute-start(f32[18,1,128]{2,1,0:T(1,128)S(1)} %get-tuple-element.21), channel_id=1, source_target_pairs={{0,1},{1,2},{2,3},{3,4},{4,5},{5,6},{6,7},{7,8},{8,9},{9,10},{10,1... | collective-permute-start | bytes 27656 | tf_op jit(solution)/shard_map/ppermute | solution.py:19
  25.0 11.2 %collective-permute-start.3 = (f32[18,1,128]{2,1,0:T(1,128)S(1)}, f32[18,1,128]{2,1,0:T(1,128)S(1)}, u32[]{:S(2)}, u32[]{:S(2)}) collective-permute-start(f32[18,1,128]{2,1,0:T(1,128)S(1)} %get-tuple-element.20), channel_id=1, source_target_pairs={{1,0},{2,1},{3,2},{4,3},{5,4},{6,5},{7,6},{8,7},{9,8},{10,9},{11,1... | collective-permute-start | bytes 27656 | tf_op jit(solution)/shard_map/ppermute | solution.py:22
  28.0 8.2 %collective-permute-start.6 = (f32[18,1,128]{2,1,0:T(1,128)S(1)}, f32[18,1,128]{2,1,0:T(1,128)S(1)}, u32[]{:S(2)}, u32[]{:S(2)}) collective-permute-start(f32[18,1,128]{2,1,0:T(1,128)S(1)} %get-tuple-element.22), channel_id=1, source_target_pairs={{0,1},{1,2},{2,3},{3,4},{4,5},{5,6},{6,7},{7,8},{8,9},{9,10},{10,1... | collective-permute-start | bytes 27656 | tf_op jit(solution)/shard_map/ppermute | solution.py:19
  32.8 6.2 %collective-permute-start.7 = (f32[18,1,128]{2,1,0:T(1,128)S(1)}, f32[18,1,128]{2,1,0:T(1,128)S(1)}, u32[]{:S(2)}, u32[]{:S(2)}) collective-permute-start(f32[18,1,128]{2,1,0:T(1,128)S(1)} %get-tuple-element.23), channel_id=1, source_target_pairs={{1,0},{2,1},{3,2},{4,3},{5,4},{6,5},{7,6},{8,7},{9,8},{10,9},{11,1... | collective-permute-start | bytes 27656 | tf_op jit(solution)/shard_map/ppermute | solution.py:22
  39.6 8.9 %collective-permute-start.8 = (f32[1,32,128]{2,1,0:T(8,128)S(1)}, f32[1,32,128]{2,1,0:T(8,128)S(1)}, u32[]{:S(2)}, u32[]{:S(2)}) collective-permute-start(f32[1,32,128]{2,1,0:T(8,128)S(1)} %get-tuple-element.38), channel_id=1, source_target_pairs={{0,16},{16,32},{32,48},{48,64},{64,80},{80,96},{96,112},{112,128},... | collective-permute-start | bytes 49160 | tf_op jit(solution)/shard_map/ppermute | solution.py:19
  46.6 7.8 %collective-permute-start.9 = (f32[1,32,128]{2,1,0:T(8,128)S(1)}, f32[1,32,128]{2,1,0:T(8,128)S(1)}, u32[]{:S(2)}, u32[]{:S(2)}) collective-permute-start(f32[1,32,128]{2,1,0:T(8,128)S(1)} %get-tuple-element.39), channel_id=1, source_target_pairs={{16,0},{32,16},{48,32},{64,48},{80,64},{96,80},{112,96},{128,112},... | collective-permute-start | bytes 49160 | tf_op jit(solution)/shard_map/ppermute | solution.py:22
  57.9 6.2 %collective-permute-start.11 = (f32[18,1,128]{2,1,0:T(1,128)S(1)}, f32[18,1,128]{2,1,0:T(1,128)S(1)}, u32[]{:S(2)}, u32[]{:S(2)}) collective-permute-start(f32[18,1,128]{2,1,0:T(1,128)S(1)} %get-tuple-element.19), channel_id=1, source_target_pairs={{1,0},{2,1},{3,2},{4,3},{5,4},{6,5},{7,6},{8,7},{9,8},{10,9},{11,1... | collective-permute-start | bytes 27656 | tf_op jit(solution)/shard_map/ppermute | solution.py:22
  64.5 40.9 %collective-permute-start.12 = (f32[1,32,128]{2,1,0:T(8,128)S(1)}, f32[1,32,128]{2,1,0:T(8,128)S(1)}, u32[]{:S(2)}, u32[]{:S(2)}) collective-permute-start(f32[1,32,128]{2,1,0:T(8,128)S(1)} %get-tuple-element.34), channel_id=1, source_target_pairs={{0,16},{16,32},{32,48},{48,64},{64,80},{80,96},{96,112},{112,128},... | collective-permute-start | bytes 49160 | tf_op jit(solution)/shard_map/ppermute | solution.py:19
  66.4 39.0 %collective-permute-start.13 = (f32[1,32,128]{2,1,0:T(8,128)S(1)}, f32[1,32,128]{2,1,0:T(8,128)S(1)}, u32[]{:S(2)}, u32[]{:S(2)}) collective-permute-start(f32[1,32,128]{2,1,0:T(8,128)S(1)} %get-tuple-element.35), channel_id=1, source_target_pairs={{16,0},{32,16},{48,32},{64,48},{80,64},{96,80},{112,96},{128,112},... | collective-permute-start | bytes 49160 | tf_op jit(solution)/shard_map/ppermute | solution.py:22
  107.9 6.2 %collective-permute-start.15 = (f32[18,1,128]{2,1,0:T(1,128)S(1)}, f32[18,1,128]{2,1,0:T(1,128)S(1)}, u32[]{:S(2)}, u32[]{:S(2)}) collective-permute-start(f32[18,1,128]{2,1,0:T(1,128)S(1)} %get-tuple-element.17), channel_id=1, source_target_pairs={{1,0},{2,1},{3,2},{4,3},{5,4},{6,5},{7,6},{8,7},{9,8},{10,9},{11,1... | collective-permute-start | bytes 27656 | tf_op jit(solution)/shard_map/ppermute | solution.py:22
  139.6 6.9 %collective-permute-start.16 = (f32[1,16,64]{2,1,0:T(8,128)S(1)}, f32[1,16,64]{2,1,0:T(8,128)S(1)}, u32[]{:S(2)}, u32[]{:S(2)}) collective-permute-start(f32[1,16,64]{2,1,0:T(8,128)S(1)} %get-tuple-element.77), channel_id=1, source_target_pairs={{0,16},{16,32},{32,48},{48,64},{64,80},{80,96},{96,112},{112,128},... | collective-permute-start | bytes 12296 | tf_op jit(solution)/shard_map/ppermute | solution.py:19
  144.6 7.7 %collective-permute-start.17 = (f32[1,16,64]{2,1,0:T(8,128)S(1)}, f32[1,16,64]{2,1,0:T(8,128)S(1)}, u32[]{:S(2)}, u32[]{:S(2)}) collective-permute-start(f32[1,16,64]{2,1,0:T(8,128)S(1)} %get-tuple-element.78), channel_id=1, source_target_pairs={{16,0},{32,16},{48,32},{64,48},{80,64},{96,80},{112,96},{128,112},... | collective-permute-start | bytes 12296 | tf_op jit(solution)/shard_map/ppermute | solution.py:22
  155.7 6.1 %collective-permute-start.19 = (f32[10,1,64]{2,1,0:T(1,128)S(1)}, f32[10,1,64]{2,1,0:T(1,128)S(1)}, u32[]{:S(2)}, u32[]{:S(2)}) collective-permute-start(f32[10,1,64]{2,1,0:T(1,128)S(1)} %get-tuple-element.55), channel_id=1, source_target_pairs={{1,0},{2,1},{3,2},{4,3},{5,4},{6,5},{7,6},{8,7},{9,8},{10,9},{11,1... | collective-permute-start | bytes 7688 | tf_op jit(solution)/shard_map/ppermute | solution.py:22
  162.0 12.7 %collective-permute-start.20 = (f32[1,16,64]{2,1,0:T(8,128)S(1)}, f32[1,16,64]{2,1,0:T(8,128)S(1)}, u32[]{:S(2)}, u32[]{:S(2)}) collective-permute-start(f32[1,16,64]{2,1,0:T(8,128)S(1)} %get-tuple-element.73), channel_id=1, source_target_pairs={{0,16},{16,32},{32,48},{48,64},{64,80},{80,96},{96,112},{112,128},... | collective-permute-start | bytes 12296 | tf_op jit(solution)/shard_map/ppermute | solution.py:19
  163.9 10.8 %collective-permute-start.21 = (f32[1,16,64]{2,1,0:T(8,128)S(1)}, f32[1,16,64]{2,1,0:T(8,128)S(1)}, u32[]{:S(2)}, u32[]{:S(2)}) collective-permute-start(f32[1,16,64]{2,1,0:T(8,128)S(1)} %get-tuple-element.74), channel_id=1, source_target_pairs={{16,0},{32,16},{48,32},{64,48},{80,64},{96,80},{112,96},{128,112},... | collective-permute-start | bytes 12296 | tf_op jit(solution)/shard_map/ppermute | solution.py:22
  188.3 6.9 %collective-permute-start.24 = (f32[1,8,32]{2,1,0:T(8,128)S(1)}, f32[1,8,32]{2,1,0:T(8,128)S(1)}, u32[]{:S(2)}, u32[]{:S(2)}) collective-permute-start(f32[1,8,32]{2,1,0:T(8,128)S(1)} %get-tuple-element.113), channel_id=1, source_target_pairs={{0,16},{16,32},{32,48},{48,64},{64,80},{80,96},{96,112},{112,128},... | collective-permute-start | bytes 3080 | tf_op jit(solution)/shard_map/ppermute | solution.py:19
  193.3 7.7 %collective-permute-start.25 = (f32[1,8,32]{2,1,0:T(8,128)S(1)}, f32[1,8,32]{2,1,0:T(8,128)S(1)}, u32[]{:S(2)}, u32[]{:S(2)}) collective-permute-start(f32[1,8,32]{2,1,0:T(8,128)S(1)} %get-tuple-element.114), channel_id=1, source_target_pairs={{16,0},{32,16},{48,32},{64,48},{80,64},{96,80},{112,96},{128,112},... | collective-permute-start | bytes 3080 | tf_op jit(solution)/shard_map/ppermute | solution.py:22
  213.3 7.7 %collective-permute-start.29 = (f32[1,8,32]{2,1,0:T(8,128)S(1)}, f32[1,8,32]{2,1,0:T(8,128)S(1)}, u32[]{:S(2)}, u32[]{:S(2)}) collective-permute-start(f32[1,8,32]{2,1,0:T(8,128)S(1)} %get-tuple-element.110), channel_id=1, source_target_pairs={{16,0},{32,16},{48,32},{64,48},{80,64},{96,80},{112,96},{128,112},... | collective-permute-start | bytes 3080 | tf_op jit(solution)/shard_map/ppermute | solution.py:22
  233.1 7.7 %collective-permute-start.33 = (f32[1,8,32]{2,1,0:T(8,128)S(1)}, f32[1,8,32]{2,1,0:T(8,128)S(1)}, u32[]{:S(2)}, u32[]{:S(2)}) collective-permute-start(f32[1,8,32]{2,1,0:T(8,128)S(1)} %get-tuple-element.106), channel_id=1, source_target_pairs={{16,0},{32,16},{48,32},{64,48},{80,64},{96,80},{112,96},{128,112},... | collective-permute-start | bytes 3080 | tf_op jit(solution)/shard_map/ppermute | solution.py:22
  252.8 7.7 %collective-permute-start.37 = (f32[1,8,32]{2,1,0:T(8,128)S(1)}, f32[1,8,32]{2,1,0:T(8,128)S(1)}, u32[]{:S(2)}, u32[]{:S(2)}) collective-permute-start(f32[1,8,32]{2,1,0:T(8,128)S(1)} %get-tuple-element.102), channel_id=1, source_target_pairs={{16,0},{32,16},{48,32},{64,48},{80,64},{96,80},{112,96},{128,112},... | collective-permute-start | bytes 3080 | tf_op jit(solution)/shard_map/ppermute | solution.py:22
  272.6 7.7 %collective-permute-start.41 = (f32[1,8,32]{2,1,0:T(8,128)S(1)}, f32[1,8,32]{2,1,0:T(8,128)S(1)}, u32[]{:S(2)}, u32[]{:S(2)}) collective-permute-start(f32[1,8,32]{2,1,0:T(8,128)S(1)} %get-tuple-element.98), channel_id=1, source_target_pairs={{16,0},{32,16},{48,32},{64,48},{80,64},{96,80},{112,96},{128,112},... | collective-permute-start | bytes 3080 | tf_op jit(solution)/shard_map/ppermute | solution.py:22
  292.3 7.7 %collective-permute-start.45 = (f32[1,8,32]{2,1,0:T(8,128)S(1)}, f32[1,8,32]{2,1,0:T(8,128)S(1)}, u32[]{:S(2)}, u32[]{:S(2)}) collective-permute-start(f32[1,8,32]{2,1,0:T(8,128)S(1)} %get-tuple-element.94), channel_id=1, source_target_pairs={{16,0},{32,16},{48,32},{64,48},{80,64},{96,80},{112,96},{128,112},... | collective-permute-start | bytes 3080 | tf_op jit(solution)/shard_map/ppermute | solution.py:22
  312.4 7.7 %collective-permute-start.49 = (f32[1,16,64]{2,1,0:T(8,128)S(1)}, f32[1,16,64]{2,1,0:T(8,128)S(1)}, u32[]{:S(2)}, u32[]{:S(2)}) collective-permute-start(f32[1,16,64]{2,1,0:T(8,128)S(1)} %get-tuple-element.63), channel_id=1, source_target_pairs={{16,0},{32,16},{48,32},{64,48},{80,64},{96,80},{112,96},{128,112},... | collective-permute-start | bytes 12296 | tf_op jit(solution)/shard_map/ppermute | solution.py:22
  331.5 7.7 %collective-permute-start.53 = (f32[1,16,64]{2,1,0:T(8,128)S(1)}, f32[1,16,64]{2,1,0:T(8,128)S(1)}, u32[]{:S(2)}, u32[]{:S(2)}) collective-permute-start(f32[1,16,64]{2,1,0:T(8,128)S(1)} %get-tuple-element.59), channel_id=1, source_target_pairs={{16,0},{32,16},{48,32},{64,48},{80,64},{96,80},{112,96},{128,112},... | collective-permute-start | bytes 12296 | tf_op jit(solution)/shard_map/ppermute | solution.py:22
  351.5 7.8 %collective-permute-start.57 = (f32[1,32,128]{2,1,0:T(8,128)S(1)}, f32[1,32,128]{2,1,0:T(8,128)S(1)}, u32[]{:S(2)}, u32[]{:S(2)}) collective-permute-start(f32[1,32,128]{2,1,0:T(8,128)S(1)} %get-tuple-element.31), channel_id=1, source_target_pairs={{16,0},{32,16},{48,32},{64,48},{80,64},{96,80},{112,96},{128,112},... | collective-permute-start | bytes 49160 | tf_op jit(solution)/shard_map/ppermute | solution.py:22
  362.5 6.2 %collective-permute-start.59 = (f32[18,1,128]{2,1,0:T(1,128)S(1)}, f32[18,1,128]{2,1,0:T(1,128)S(1)}, u32[]{:S(2)}, u32[]{:S(2)}) collective-permute-start(f32[18,1,128]{2,1,0:T(1,128)S(1)} %get-tuple-element.15), channel_id=1, source_target_pairs={{1,0},{2,1},{3,2},{4,3},{5,4},{6,5},{7,6},{8,7},{9,8},{10,9},{11,1... | collective-permute-start | bytes 27656 | tf_op jit(solution)/shard_map/ppermute | solution.py:22
  371.0 7.8 %collective-permute-start.61 = (f32[1,32,128]{2,1,0:T(8,128)S(1)}, f32[1,32,128]{2,1,0:T(8,128)S(1)}, u32[]{:S(2)}, u32[]{:S(2)}) collective-permute-start(f32[1,32,128]{2,1,0:T(8,128)S(1)} %get-tuple-element.27), channel_id=1, source_target_pairs={{16,0},{32,16},{48,32},{64,48},{80,64},{96,80},{112,96},{128,112},... | collective-permute-start | bytes 49160 | tf_op jit(solution)/shard_map/ppermute | solution.py:22
  381.9 6.2 %collective-permute-start.63 = (f32[18,1,128]{2,1,0:T(1,128)S(1)}, f32[18,1,128]{2,1,0:T(1,128)S(1)}, u32[]{:S(2)}, u32[]{:S(2)}) collective-permute-start(f32[18,1,128]{2,1,0:T(1,128)S(1)} %get-tuple-element.13), channel_id=1, source_target_pairs={{1,0},{2,1},{3,2},{4,3},{5,4},{6,5},{7,6},{8,7},{9,8},{10,9},{11,1... | collective-permute-start | bytes 27656 | tf_op jit(solution)/shard_map/ppermute | solution.py:22
  (56 other events, 1810.8 us)
where the time goes:
time: 392 us; the launch traced here: 389 us
  starting transfers between devices  182 us (46%)
  waiting for transfers between devices  116 us (30%)
  local copies, waits for them, and re-layouts  58.1 us (15%)
  other arithmetic  30.7 us (8%)
    ppermute x32, waiting for transfers between devices, padded_2(): lax.ppermute(lax.slice_in_dim(block, 0, width, axis=dim), axis, backward)  116 us
    ppermute x32, starting transfers between devices, padded_2(): lax.ppermute(lax.slice_in_dim(block, block.shape[dim] - width, None, axis...  104 us
    ppermute x32, starting transfers between devices, padded_2(): lax.ppermute(lax.slice_in_dim(block, 0, width, axis=dim), axis, backward)  78 us
    reshape x2, local copies, waits for them, and re-layouts, coarsen_cells(): value.reshape(ext_x // 2, 2, ext_y // 2, 2, ext_z // 2, 2)  21.1 us
    add x13, other arithmetic, sweep(): return field + invd * (rhs_level - apply_operator(padded, coefs, scale))  8.05 us
  transfers between devices with their start and end apart: 64, of which 27 were waited for; matrix products, arithmetic and copies ran while one was open for 12% of the time, Pallas kernels for 0%

commit v1 on v0

v1 whole, which is shorter than its diff:
```python
import functools

import jax
import jax.numpy as jnp
from jax import lax
from jax.experimental import pallas as pl
from jax.experimental.pallas import tpu as pltpu
from jax.sharding import PartitionSpec as P

MESH = pl.DeviceIdType.MESH
PRE = 2
POST = 2
COARSE_SWEEPS = 6
WEIGHT = 0.8
KEEP = 1.0 - WEIGHT

DIRS = [(dx, dy) for dx in (-1, 0, 1) for dy in (-1, 0, 1) if (dx, dy) != (0, 0)]
FAR = [(dx, dy) for dx in (-2, -1, 0, 1, 2) for dy in (-1, 0, 1) if (dx, dy) != (0, 0)]


def send_range(step, first, count, width):
    if step == 0:
        return pl.ds(first, count)
    return pl.ds(first + count - width, width) if step > 0 else pl.ds(first, width)


def planes_to(step, first, count, width):
    if step == 0:
        return pl.ds(first, count)
    return pl.ds(first - width, width) if step > 0 else pl.ds(first + count, width)


def rows_to(step, count, width):
    if step == 0:
        return pl.ds(0, count)
    return pl.ds(count + width, width) if step > 0 else pl.ds(count, width)


def lanes(shape):
    return lax.broadcasted_iota(jnp.int32, shape, len(shape) - 1)


def roll_z(value, shift):
    return pltpu.roll(value, shift % 128, value.ndim - 1)


def roll_y(value, shift):
    return pltpu.roll(value, shift % value.shape[-2], value.ndim - 2)


def pack_pairs(value):
    split = value.reshape((value.shape[0] // 2, 2) + value.shape[1:])
    even, odd = split[:, 0], split[:, 1]
    mask = lanes(even.shape) % 2 == 0
    return jnp.where(mask, even + roll_z(even, -1), odd + roll_z(odd, 1))


def pack_groups(value):
    lane = lanes(value.shape[1:])
    low = jnp.where(lane % 2 == 0, value[0] + roll_z(value[0], -1), value[1] + roll_z(value[1], 1))
    high = jnp.where(lane % 2 == 0, value[2] + roll_z(value[2], -1), value[3] + roll_z(value[3], 1))
    return jnp.where(lane % 4 < 2, low + roll_z(low, -2), high + roll_z(high, 2))


def spread_pairs(value):
    mask = lanes(value.shape) % 2 == 0
    return jnp.where(mask, value, roll_z(value, 1)), jnp.where(mask, roll_z(value, -1), value)


def spread_groups(value):
    mask = lanes(value.shape) % 4 < 2
    low = jnp.where(mask, value, roll_z(value, 2))
    high = jnp.where(mask, roll_z(value, -2), value)
    return spread_pairs(low) + spread_pairs(high)


def ahead(value):
    return jnp.concatenate([value[1:], value[:1]], axis=0)


def behind(value):
    return jnp.concatenate([value[-1:], value[:-1]], axis=0)


def x_up(value, following, group):
    mask = lanes(value.shape) % group < group - 1
    return jnp.where(mask, roll_z(value, -1), roll_z(following, group - 1))


def x_down(value, previous, group):
    mask = lanes(value.shape) % group > 0
    return jnp.where(mask, roll_z(value, 1), roll_z(previous, 1 - group))


def coarse_weights(w, faces, inv, group, scale):
    half = scale * inv
    w[0] = half * faces[0]
    w[1] = half * x_up(faces[0], ahead(faces[0]), group)
    w[2] = half * faces[1]
    w[3] = half * roll_y(faces[1], -1)
    w[4] = half * faces[2]
    w[5] = half * roll_z(faces[2], -group)


def coarse_sum(w, value, group):
    total = w[0] * x_down(value, behind(value), group) + w[1] * x_up(value, ahead(value), group)
    total = total + w[2] * roll_y(value, 1) + w[3] * roll_y(value, -1)
    return total + w[4] * roll_z(value, group) + w[5] * roll_z(value, -group)


def kernel(
    sizes, p_hbm, s_hbm, d_hbm, o_hbm,
    p, d, s, v1, v2, fh, out, w0, g0, dg0,
    xs, ys, cs, l1, w1, b1, dg1, c2, w2, b2, e1, e0,
    local_sem, d_sem, p_sem, s_sem, f_sem, l1_sem, b1_sem, c2_sem, b2_sem,
):
    n_blk, n_sub = sizes
    ib, iy = lax.axis_index("blk"), lax.axis_index("sub")

    def peer(dx, dy):
        return {"blk": lax.rem(ib + (dx + n_blk), n_blk), "sub": lax.rem(iy + (dy + n_sub), n_sub)}

    def remote(src, dst, sem, k, dx, dy):
        return pltpu.make_async_remote_copy(
            src_ref=src, dst_ref=dst, send_sem=sem.at[0, k], recv_sem=sem.at[1, k],
            device_id=peer(dx, dy), device_id_type=MESH,
        )

    local = [
        pltpu.make_async_copy(src, dst.at[pl.ds(3, 16), pl.ds(0, 32)], local_sem.at[k])
        for k, (src, dst) in enumerate(((d_hbm, d), (p_hbm, p), (s_hbm, s)))
    ]
    for copy in local:
        copy.start()
    barrier = pltpu.get_barrier_semaphore()
    for dx, dy in FAR:
        pl.semaphore_signal(barrier, inc=1, device_id=peer(dx, dy), device_id_type=MESH)
    for copy in local:
        copy.wait()
    pl.semaphore_wait(barrier, len(FAR))

    def fine_copies(src, dst, sem, width):
        return [
            remote(
                src.at[send_range(dx, 3, 16, width), send_range(dy, 0, 32, 4)],
                dst.at[planes_to(dx, 3, 16, width), rows_to(dy, 32, 4)],
                sem, k, dx, dy,
            )
            for k, (dx, dy) in enumerate(DIRS)
        ]

    d_copies = fine_copies(d, d, d_sem, 3)
    p_copies = fine_copies(p, p, p_sem, 3)
    s_copies = fine_copies(s, s, s_sem, 2)
    for copy in d_copies + p_copies + s_copies:
        copy.start()

    def clear_fine(ref):
        zero = jnp.zeros((3, 40, 128), jnp.float32)
        strip = jnp.zeros((22, 4, 128), jnp.float32)

        @pl.when(ib == 0)
        def _():
            ref[0:3] = zero

        @pl.when(ib == n_blk - 1)
        def _():
            ref[19:22] = zero

        @pl.when(iy == 0)
        def _():
            ref[:, 36:40] = strip

        @pl.when(iy == n_sub - 1)
        def _():
            ref[:, 32:36] = strip

    for copy in d_copies:
        copy.wait_recv()
    clear_fine(d)

    def x_face(i, _):
        xs[i] = d[2 * i + 2, 0:32] + d[2 * i + 3, 0:32]
        return 0

    lax.fori_loop(0, 10, x_face, 0, unroll=True)

    def x_pair(i, _):
        both = d[2 * i + 3] + d[2 * i + 4]
        ys[i, 0:8] = both[32:40]
        ys[i, 8:48] = both
        return 0

    lax.fori_loop(0, 8, x_pair, 0, unroll=True)

    lane1 = lanes((4, 16, 128))
    faces_x = 0.125 * pack_pairs(xs[:, pl.ds(0, 16, stride=2), :] + xs[:, pl.ds(1, 16, stride=2), :])
    lx = faces_x[0:4]
    ux = x_up(lx, faces_x[1:5], 2)
    odd_before = ys[:, pl.ds(7, 16, stride=2), :]
    even = ys[:, pl.ds(8, 16, stride=2), :]
    odd = ys[:, pl.ds(9, 16, stride=2), :]
    even_after = ys[:, pl.ds(10, 16, stride=2), :]
    ly = 0.125 * pack_pairs(even + odd_before)
    uy = 0.125 * pack_pairs(odd + even_after)
    both = (even + odd).reshape(4, 2, 16, 128)
    b_even, b_odd = both[:, 0], both[:, 1]
    first, last = lane1 < 2, lane1 >= 126
    zero1 = jnp.zeros((4, 16, 128), jnp.float32)
    is_even = lane1 % 2 == 0
    lz = 0.125 * (
        jnp.where(is_even, b_even, roll_z(b_odd, 1))
        + jnp.where(first, zero1, jnp.where(is_even, roll_z(b_even, 1), roll_z(b_odd, 2)))
    )
    uz = 0.125 * (
        jnp.where(is_even, roll_z(b_even, -1), b_odd)
        + jnp.where(last, zero1, jnp.where(is_even, roll_z(b_even, -2), roll_z(b_odd, -1)))
    )
    diag1 = 0.25 * (lx + ux + ly + uy + lz + uz)
    dg1[...] = diag1 * (1.0 / WEIGHT)
    l1[0, 2:6, 0:16] = lx
    l1[1, 2:6, 0:16] = ly
    l1[2, 2:6, 0:16] = jnp.where(first, zero1, lz)
    l1[3, 2:6, 0:16] = WEIGHT / diag1

    l1_copies = [
        remote(
            l1.at[:, send_range(dx, 2, 4, 2), send_range(dy, 0, 16, 4)],
            l1.at[:, planes_to(dx, 2, 4, 2), rows_to(dy, 16, 4)],
            l1_sem, k, dx, dy,
        )
        for k, (dx, dy) in enumerate(DIRS)
    ]
    for copy in l1_copies:
        copy.start()

    for k, face in enumerate((lx, ux, ly, uy, lz, uz)):
        cs[k] = face

    def rows_of(k, parity):
        return cs[k, :, pl.ds(parity, 8, stride=2), :]

    lane2 = lanes((4, 8, 128))
    zero2 = jnp.zeros((4, 8, 128), jnp.float32)
    lx2 = jnp.where(lane2 % 2 == 0, rows_of(0, 0) + rows_of(0, 1), zero2)
    ux2 = jnp.where(lane2 % 2 == 1, rows_of(1, 0) + rows_of(1, 1), zero2)
    ly2 = rows_of(2, 0)
    uy2 = rows_of(3, 1)
    lz2 = jnp.where(lane2 % 4 < 2, rows_of(4, 0) + rows_of(4, 1), zero2)
    uz2 = jnp.where(lane2 % 4 >= 2, rows_of(5, 0) + rows_of(5, 1), zero2)
    diag2 = (0.0625 * 0.25) * pack_groups(lx2 + ux2 + ly2 + uy2 + lz2 + uz2)
    c2[0, 2, 8:16] = 0.25 * pack_groups(lx2)
    c2[1, 2, 8:16] = 0.25 * pack_groups(ly2)
    c2[2, 2, 8:16] = jnp.where(lanes((8, 128)) < 4, 0.0, 0.25 * pack_groups(lz2))
    c2[3, 2, 8:16] = WEIGHT / diag2

    c2_copies = [
        remote(
            c2.at[:, 2, pl.ds(8, 8)], c2.at[:, 2 - dx, pl.ds(8 - 8 * dy, 8)], c2_sem, k, dx, dy
        )
        for k, (dx, dy) in enumerate(FAR)
    ]
    for copy in c2_copies:
        copy.start()

    lane0 = lanes((40, 128))
    zero0 = jnp.zeros((40, 128), jnp.float32)

    def fine_weights(i, carry):
        below, here = carry
        above = d[i + 1]
        row_below, row_above = roll_y(here, 1), roll_y(here, -1)
        z_below = jnp.where(lane0 > 0, roll_z(here, 1), zero0)
        z_above = jnp.where(lane0 < 127, roll_z(here, -1), zero0)
        near = (below + above) + (row_below + row_above) + (z_below + z_above)
        diag = 3.0 * here + 0.5 * near
        inv = jnp.where(here > 0.0, WEIGHT / diag, zero0)
        half = 0.5 * inv
        w0[0, i] = half * (here + below)
        w0[1, i] = half * (here + above)
        w0[2, i] = half * (here + row_below)
        w0[3, i] = half * (here + row_above)
        w0[4, i] = jnp.where(lane0 > 0, half * (here + z_below), zero0)
        w0[5, i] = jnp.where(lane0 < 127, half * (here + z_above), zero0)
        g0[i] = inv
        dg0[i] = diag * (1.0 / WEIGHT)
        return here, above

    lax.fori_loop(1, 21, fine_weights, (d[0], d[1]), unroll=True)

    for copy in p_copies + s_copies:
        copy.wait_recv()
    clear_fine(p)

    def scale_source(i, _):
        g0[i] = g0[i] * s[i]
        return 0

    lax.fori_loop(1, 21, scale_source, 0, unroll=True)

    def fine_sum(i, below, here, above):
        total = g0[i] + w0[0, i] * below + w0[1, i] * above
        total = total + w0[2, i] * roll_y(here, 1) + w0[3, i] * roll_y(here, -1)
        return total + w0[4, i] * roll_z(here, 1) + w0[5, i] * roll_z(here, -1)

    def fine_sweep(src, dst, low, high):
        def plane(i, carry):
            below, here = carry
            above = src[i + 1]
            dst[i] = fine_sum(i, below, here, above) + KEEP * here
            return here, above

        lax.fori_loop(low, high, plane, (src[low - 1], src[low]), unroll=True)

    fine_sweep(p, v1, 1, 21)
    fine_sweep(v1, v2, 2, 20)

    def residual(pair, carry):
        below, here = carry
        above = v2[2 * pair + 4]
        beyond = v2[2 * pair + 5]
        first_half = (fine_sum(2 * pair + 3, below, here, above) - WEIGHT * here) * dg0[2 * pair + 3]
        second_half = (fine_sum(2 * pair + 4, here, above, beyond) - WEIGHT * above) * dg0[2 * pair + 4]
        xs[pair] = (first_half + second_half)[0:32]
        return above, beyond

    lax.fori_loop(0, 8, residual, (v2[2], v2[3]), unroll=True)
    b1[2:6, 0:16] = 0.125 * pack_pairs(
        xs[0:8, pl.ds(0, 16, stride=2), :] + xs[0:8, pl.ds(1, 16, stride=2), :]
    )
    b1_copies = [
        remote(
            b1.at[send_range(dx, 2, 4, 2), send_range(dy, 0, 16, 4)],
            b1.at[planes_to(dx, 2, 4, 2), rows_to(dy, 16, 4)],
            b1_sem, k, dx, dy,
        )
        for k, (dx, dy) in enumerate(DIRS)
    ]
    f_copies = fine_copies(v2, fh, f_sem, 2)
    for copy in b1_copies + f_copies:
        copy.start()

    for copy in l1_copies:
        copy.wait_recv()
    pairs = jnp.zeros((2, 24, 128), jnp.float32)
    strip1 = jnp.zeros((8, 4, 128), jnp.float32)

    @pl.when(ib == 0)
    def _():
        l1[3, 0:2] = pairs

    @pl.when(ib == n_blk - 1)
    def _():
        l1[3, 6:8] = pairs

    @pl.when(iy == 0)
    def _():
        l1[3, :, 20:24] = strip1

    @pl.when(iy == n_sub - 1)
    def _():
        l1[3, :, 16:20] = strip1

    inv1 = l1[3]
    coarse_weights(w1, l1, inv1, 2, 0.25)

    for copy in c2_copies:
        copy.wait_recv()
    group = jnp.zeros((24, 128), jnp.float32)
    strip2 = jnp.zeros((5, 8, 128), jnp.float32)

    for index in range(5):
        @pl.when((ib + (index - 2) < 0) | (ib + (index - 2) >= n_blk))
        def _():
            c2[3, index] = group

    @pl.when(iy == 0)
    def _():
        c2[3, :, 0:8] = strip2

    @pl.when(iy == n_sub - 1)
    def _():
        c2[3, :, 16:24] = strip2

    inv2 = c2[3]
    coarse_weights(w2, c2, inv2, 4, 0.0625)

    for copy in b1_copies:
        copy.wait_recv()
    g1 = l1[3] * b1[...]
    err1 = g1
    err1 = g1 + coarse_sum(w1, err1, 2) + KEEP * err1
    res1 = (g1 + coarse_sum(w1, err1, 2) - WEIGHT * err1)[2:6, 0:16] * dg1[...]
    xs[0:4, 0:16] = res1
    b2[2, 8:16] = 0.125 * pack_groups(
        xs[0:4, pl.ds(0, 8, stride=2), :] + xs[0:4, pl.ds(1, 8, stride=2), :]
    )
    b2_copies = [
        remote(b2.at[2, pl.ds(8, 8)], b2.at[2 - dx, pl.ds(8 - 8 * dy, 8)], b2_sem, k, dx, dy)
        for k, (dx, dy) in enumerate(FAR)
    ]
    for copy in b2_copies:
        copy.start()
    for copy in b2_copies:
        copy.wait_recv()
    g2 = c2[3] * b2[...]
    err2 = g2
    for _ in range(COARSE_SWEEPS):
        err2 = g2 + coarse_sum(w2, err2, 4) + KEEP * err2

    row = lax.broadcasted_iota(jnp.int32, (8, 128), 0)

    def put(pair, value):
        centre = value[8:16]
        sides = jnp.where(row < 2, value[16:24], roll_y(value[0:8], 4))
        for parity in range(2):
            e1[pair, pl.ds(parity, 8, stride=2), :] = centre
            e1[pair, pl.ds(16 + parity, 8, stride=2), :] = sides

    before, centre, after = spread_groups(err2[1]), spread_groups(err2[2]), spread_groups(err2[3])
    for pair, value in enumerate(before[2:4] + centre + after[0:2]):
        put(pair, value)
    g1 = l1[3] * b1[...]
    err1 = err1 + e1[:, 0:24]
    for _ in range(POST):
        err1 = g1 + coarse_sum(w1, err1, 2) + KEEP * err1

    def put_fine(index, value):
        sides = jnp.where(row < 2, value[16:24], roll_y(value[16:24], 4))
        for parity in range(2):
            e0[index, pl.ds(parity, 16, stride=2), :] = value[0:16]
            e0[index, pl.ds(32 + parity, 8, stride=2), :] = sides

    for pair in range(1, 7):
        even_cell, odd_cell = spread_pairs(err1[pair])
        if pair > 1:
            put_fine(2 * pair - 3, even_cell)
        if pair < 6:
            put_fine(2 * pair - 2, odd_cell)

    for copy in f_copies:
        copy.wait_recv()
    clear_fine(fh)

    def correct(i, _):
        halves = (2 * i + 1, 2 * i + 2)
        add = e0[i]
        for plane in halves:
            v1[plane, 0:32] = v2[plane, 0:32] + add[0:32]
            v1[plane, 32:40] = fh[plane, 32:40] + add[32:40]
        return 0

    for i in (0, 9):
        for plane in (2 * i + 1, 2 * i + 2):
            v1[plane] = fh[plane] + e0[i, 0:40]
    lax.fori_loop(1, 9, correct, 0, unroll=True)

    fine_sweep(v1, fh, 2, 20)

    def last_sweep(i, carry):
        below, here = carry
        above = fh[i + 1]
        out[i - 3] = (fine_sum(i, below, here, above) + KEEP * here)[0:32]
        return here, above

    lax.fori_loop(3, 19, last_sweep, (fh[2], fh[3]), unroll=True)
    store = pltpu.make_async_copy(out, o_hbm, local_sem.at[3])
    store.start()
    for copy in d_copies + p_copies + s_copies + l1_copies + c2_copies + f_copies + b1_copies + b2_copies:
        copy.wait_send()
    store.wait()


def solution(mesh):
    sizes = (mesh.shape["blk"], mesh.shape["sub"])

    def on_device(pressure, source, inv_density):
        def vmem(*shape):
            return pltpu.VMEM(shape, jnp.float32)

        near, far = len(DIRS), len(FAR)
        return pl.pallas_call(
            functools.partial(kernel, sizes),
            out_shape=jax.ShapeDtypeStruct((16, 32, 128), jnp.float32),
            in_specs=[pl.BlockSpec(memory_space=pl.ANY)] * 3,
            out_specs=pl.BlockSpec(memory_space=pl.ANY),
            scratch_shapes=[
                vmem(22, 40, 128), vmem(22, 40, 128), vmem(22, 40, 128),
                vmem(22, 40, 128), vmem(22, 40, 128), vmem(22, 40, 128),
                vmem(16, 32, 128), vmem(6, 22, 40, 128), vmem(22, 40, 128), vmem(22, 40, 128),
                vmem(10, 32, 128), vmem(8, 48, 128), vmem(6, 4, 16, 128),
                vmem(4, 8, 24, 128), vmem(6, 8, 24, 128), vmem(8, 24, 128), vmem(4, 16, 128),
                vmem(4, 5, 24, 128), vmem(6, 5, 24, 128), vmem(5, 24, 128),
                vmem(8, 32, 128), vmem(10, 48, 128),
                pltpu.SemaphoreType.DMA((4,)),
                pltpu.SemaphoreType.DMA((2, near)), pltpu.SemaphoreType.DMA((2, near)),
                pltpu.SemaphoreType.DMA((2, near)), pltpu.SemaphoreType.DMA((2, near)),
                pltpu.SemaphoreType.DMA((2, near)), pltpu.SemaphoreType.DMA((2, near)),
                pltpu.SemaphoreType.DMA((2, far)), pltpu.SemaphoreType.DMA((2, far)),
            ],
            compiler_params=pltpu.CompilerParams(
                collective_id=0, has_side_effects=True, vmem_limit_bytes=32 * 1024 * 1024
            ),
        )(pressure, source, inv_density)

    return jax.shard_map(
        on_device,
        mesh=mesh,
        in_specs=(P("blk", "sub", None),) * 3,
        out_specs=P("blk", "sub", None),
        check_vma=False,
    )
```

time: 392 us -> 50.3 us (0.13)
  the two profiles are of different devices: /device:TPU:447 before, /device:TPU:1 now
where the time goes in v1:
time: 50.3 us; the launch traced here: 50.1 us
  Pallas kernels  46.6 us (93%)
  local copies, waits for them, and re-layouts  3.55 us (7%)
    pallas_call x1, Pallas kernels, on_device(): pl.pallas_call(functools.partial(kernel, sizes), out_shape=jax.ShapeDtype...  46.6 us
    unnamed x7, local copies, waits for them, and re-layouts  3.55 us

profile of v1, /device:TPU:1, one launch (start us, length us, event | category | flops | bytes accessed | tf_op | source)
XLA Modules:
  0.0 50.1 jit_solution(17680721222636200786)
XLA Ops:
  0.0 0.0 copy-start
  0.0 0.9 %copy-done = f32[16,32,128]{2,1,0:T(8,128)S(1)} copy-done((f32[16,32,128]{2,1,0:T(8,128)S(1)}, f32[16,32,128]{2,1,0:T(8,128)}, u32[]{:S(2)}) %copy-start) | copy-done | bytes 262168
  1.0 0.0 copy-start.1
  1.0 0.9 %copy-done.1 = f32[16,32,128]{2,1,0:T(8,128)S(1)} copy-done((f32[16,32,128]{2,1,0:T(8,128)S(1)}, f32[16,32,128]{2,1,0:T(8,128)}, u32[]{:S(2)}) %copy-start.1) | copy-done | bytes 262168
  1.9 0.0 copy-start.2
  1.9 0.9 %copy-done.2 = f32[16,32,128]{2,1,0:T(8,128)S(1)} copy-done((f32[16,32,128]{2,1,0:T(8,128)S(1)}, f32[16,32,128]{2,1,0:T(8,128)}, u32[]{:S(2)}) %copy-start.2) | copy-done | bytes 262168
  2.9 46.6 %shard_map.37 = f32[16,32,128]{2,1,0:T(8,128)S(1)} custom-call(f32[16,32,128]{2,1,0:T(8,128)S(1)} %copy-done, f32[16,32,128]{2,1,0:T(8,128)S(1)} %copy-done.1, f32[16,32,128]{2,1,0:T(8,128)S(1)} %copy-done.2), custom_call_target="tpu_custom_call" | custom-call | tf_op jit(solution)/shard_map/pallas_call | solution.py:482
  49.4 0.7 %copy.5 = f32[16,32,128]{2,1,0:T(8,128)} copy(f32[16,32,128]{2,1,0:T(8,128)S(1)} %shard_map.37) | data formatting | bytes 524288
Async XLA Ops:
  0.0 0.9 %copy-start = (f32[16,32,128]{2,1,0:T(8,128)S(1)}, f32[16,32,128]{2,1,0:T(8,128)}, u32[]{:S(2)}) copy-start(f32[16,32,128]{2,1,0:T(8,128)} %p_hbm.1) | copy-start | bytes 786436
  1.0 0.9 %copy-start.1 = (f32[16,32,128]{2,1,0:T(8,128)S(1)}, f32[16,32,128]{2,1,0:T(8,128)}, u32[]{:S(2)}) copy-start(f32[16,32,128]{2,1,0:T(8,128)} %s_hbm.1) | copy-start | bytes 786436
  1.9 0.9 %copy-start.2 = (f32[16,32,128]{2,1,0:T(8,128)S(1)}, f32[16,32,128]{2,1,0:T(8,128)}, u32[]{:S(2)}) copy-start(f32[16,32,128]{2,1,0:T(8,128)} %d_hbm.1) | copy-start | bytes 786436

commit v2 on v1

--- a/solution.py
+++ b/solution.py
@@ -14,8 +14,8 @@
 WEIGHT = 0.8
 KEEP = 1.0 - WEIGHT
 
-DIRS = [(dx, dy) for dx in (-1, 0, 1) for dy in (-1, 0, 1) if (dx, dy) != (0, 0)]
-FAR = [(dx, dy) for dx in (-2, -1, 0, 1, 2) for dy in (-1, 0, 1) if (dx, dy) != (0, 0)]
+DIRS = [(-1, -1), (1, 1), (-1, 1), (1, -1), (-1, 0), (1, 0), (0, -1), (0, 1)]
+FAR = [(-2, -1), (2, 1), (-2, 1), (2, -1), (-2, 0), (2, 0)] + DIRS
 
 
 def send_range(step, first, count, width):
@@ -34,6 +34,12 @@
     if step == 0:
         return pl.ds(0, count)
     return pl.ds(count + width, width) if step > 0 else pl.ds(count, width)
+
+
+def far_rows(dx, dy, shift):
+    if abs(dx) + abs(dy) == 3:
+        return pl.ds(8 + shift + (4 if dy > 0 else 0), 4)
+    return pl.ds(8 + shift, 8)
 
 
 def lanes(shape):
@@ -133,17 +139,17 @@
     for copy in local:
         copy.start()
     barrier = pltpu.get_barrier_semaphore()
-    for dx, dy in FAR:
+    for dx, dy in DIRS:
         pl.semaphore_signal(barrier, inc=1, device_id=peer(dx, dy), device_id_type=MESH)
     for copy in local:
         copy.wait()
-    pl.semaphore_wait(barrier, len(FAR))
+    pl.semaphore_wait(barrier, len(DIRS))
 
     def fine_copies(src, dst, sem, width):
         return [
             remote(
-                src.at[send_range(dx, 3, 16, width), send_range(dy, 0, 32, 4)],
-                dst.at[planes_to(dx, 3, 16, width), rows_to(dy, 32, 4)],
+                src.at[send_range(dx, 3, 16, width - abs(dy)), send_range(dy, 0, 32, 4)],
+                dst.at[planes_to(dx, 3, 16, width - abs(dy)), rows_to(dy, 32, 4)],
                 sem, k, dx, dy,
             )
             for k, (dx, dy) in enumerate(DIRS)
@@ -256,13 +262,11 @@
 
     c2_copies = [
         remote(
-            c2.at[:, 2, pl.ds(8, 8)], c2.at[:, 2 - dx, pl.ds(8 - 8 * dy, 8)], c2_sem, k, dx, dy
+            c2.at[:, 2, far_rows(dx, dy, 0)], c2.at[:, 2 - dx, far_rows(dx, dy, -8 * dy)],
+            c2_sem, k, dx, dy,
         )
         for k, (dx, dy) in enumerate(FAR)
     ]
-    for copy in c2_copies:
-        copy.start()
-
     lane0 = lanes((40, 128))
     zero0 = jnp.zeros((40, 128), jnp.float32)
 
@@ -337,7 +341,7 @@
         for k, (dx, dy) in enumerate(DIRS)
     ]
     f_copies = fine_copies(v2, fh, f_sem, 2)
-    for copy in b1_copies + f_copies:
+    for copy in b1_copies + c2_copies:
         copy.start()
 
     for copy in l1_copies:
@@ -363,27 +367,6 @@
 
     inv1 = l1[3]
     coarse_weights(w1, l1, inv1, 2, 0.25)
-
-    for copy in c2_copies:
-        copy.wait_recv()
-    group = jnp.zeros((24, 128), jnp.float32)
-    strip2 = jnp.zeros((5, 8, 128), jnp.float32)
-
-    for index in range(5):
-        @pl.when((ib + (index - 2) < 0) | (ib + (index - 2) >= n_blk))
-        def _():
-            c2[3, index] = group
-
-    @pl.when(iy == 0)
-    def _():
-        c2[3, :, 0:8] = strip2
-
-    @pl.when(iy == n_sub - 1)
-    def _():
-        c2[3, :, 16:24] = strip2
-
-    inv2 = c2[3]
-    coarse_weights(w2, c2, inv2, 4, 0.0625)
 
     for copy in b1_copies:
         copy.wait_recv()
@@ -396,11 +379,35 @@
         xs[0:4, pl.ds(0, 8, stride=2), :] + xs[0:4, pl.ds(1, 8, stride=2), :]
     )
     b2_copies = [
-        remote(b2.at[2, pl.ds(8, 8)], b2.at[2 - dx, pl.ds(8 - 8 * dy, 8)], b2_sem, k, dx, dy)
+        remote(
+            b2.at[2, far_rows(dx, dy, 0)], b2.at[2 - dx, far_rows(dx, dy, -8 * dy)],
+            b2_sem, k, dx, dy,
+        )
         for k, (dx, dy) in enumerate(FAR)
     ]
-    for copy in b2_copies:
+    for copy in b2_copies + f_copies:
         copy.start()
+    for copy in c2_copies:
+        copy.wait_recv()
+    group = jnp.zeros((24, 128), jnp.float32)
+    strip2 = jnp.zeros((5, 8, 128), jnp.float32)
+
+    for index in range(5):
+        @pl.when((ib + (index - 2) < 0) | (ib + (index - 2) >= n_blk))
+        def _():
+            c2[3, index] = group
+
+    @pl.when(iy == 0)
+    def _():
+        c2[3, :, 0:8] = strip2
+
+    @pl.when(iy == n_sub - 1)
+    def _():
+        c2[3, :, 16:24] = strip2
+
+    inv2 = c2[3]
+    coarse_weights(w2, c2, inv2, 4, 0.0625)
+
     for copy in b2_copies:
         copy.wait_recv()
     g2 = c2[3] * b2[...]
@@ -463,12 +470,17 @@
         out[i - 3] = (fine_sum(i, below, here, above) + KEEP * here)[0:32]
         return here, above
 
-    lax.fori_loop(3, 19, last_sweep, (fh[2], fh[3]), unroll=True)
-    store = pltpu.make_async_copy(out, o_hbm, local_sem.at[3])
-    store.start()
+    carry = (fh[2], fh[3])
+    stores = []
+    for k in range(4):
+        carry = lax.fori_loop(4 * k + 3, 4 * k + 7, last_sweep, carry, unroll=True)
+        part = pl.ds(4 * k, 4)
+        stores.append(pltpu.make_async_copy(out.at[part], o_hbm.at[part], local_sem.at[3 + k]))
+        stores[-1].start()
     for copy in d_copies + p_copies + s_copies + l1_copies + c2_copies + f_copies + b1_copies + b2_copies:
         copy.wait_send()
-    store.wait()
+    for store in stores:
+        store.wait()
 
 
 def solution(mesh):
@@ -482,7 +494,7 @@
         return pl.pallas_call(
             functools.partial(kernel, sizes),
             out_shape=jax.ShapeDtypeStruct((16, 32, 128), jnp.float32),
-            in_specs=[pl.BlockSpec(memory_space=pl.ANY)] * 3,
+            in_specs=[pl.BlockSpec(memory_space=pltpu.HBM)] * 3,
             out_specs=pl.BlockSpec(memory_space=pl.ANY),
             scratch_shapes=[
                 vmem(22, 40, 128), vmem(22, 40, 128), vmem(22, 40, 128),
@@ -492,14 +504,14 @@
                 vmem(4, 8, 24, 128), vmem(6, 8, 24, 128), vmem(8, 24, 128), vmem(4, 16, 128),
                 vmem(4, 5, 24, 128), vmem(6, 5, 24, 128), vmem(5, 24, 128),
                 vmem(8, 32, 128), vmem(10, 48, 128),
-                pltpu.SemaphoreType.DMA((4,)),
+                pltpu.SemaphoreType.DMA((7,)),
                 pltpu.SemaphoreType.DMA((2, near)), pltpu.SemaphoreType.DMA((2, near)),
                 pltpu.SemaphoreType.DMA((2, near)), pltpu.SemaphoreType.DMA((2, near)),
                 pltpu.SemaphoreType.DMA((2, near)), pltpu.SemaphoreType.DMA((2, near)),
                 pltpu.SemaphoreType.DMA((2, far)), pltpu.SemaphoreType.DMA((2, far)),
             ],
             compiler_params=pltpu.CompilerParams(
-                collective_id=0, has_side_effects=True, vmem_limit_bytes=32 * 1024 * 1024
+                collective_id=0, has_side_effects=True, vmem_limit_bytes=54850 * 1024
             ),
         )(pressure, source, inv_density)
 

time: 50.3 us -> 43.6 us (0.87)
  Pallas kernels: 46.6 us -> 42.7 us
  local copies, waits for them, and re-layouts: 3.55 us -> 0.71 us
    pallas_call x1, Pallas kernels: 46.6 us -> 42.7 us  [on_device(): pl.pallas_call(functools.partial(kernel, sizes), out_shape=jax.ShapeDtype...]
    unnamed x7 -> x1, local copies, waits for them, and re-layouts: 3.55 us -> 0.71 us
where the time goes in v2:
time: 43.6 us; the launch traced here: 43.4 us
  Pallas kernels  42.7 us (98%)
  local copies, waits for them, and re-layouts  0.71 us (2%)
    pallas_call x1, Pallas kernels, on_device(): pl.pallas_call(functools.partial(kernel, sizes), out_shape=jax.ShapeDtype...  42.7 us

profile of v2, /device:TPU:1, one launch (start us, length us, event | category | flops | bytes accessed | tf_op | source)
XLA Modules:
  0.0 43.4 jit_solution(12650941287824845805)
XLA Ops:
  0.0 42.7 %shard_map.37 = f32[16,32,128]{2,1,0:T(8,128)S(1)} custom-call(f32[16,32,128]{2,1,0:T(8,128)} %p_hbm.1, f32[16,32,128]{2,1,0:T(8,128)} %s_hbm.1, f32[16,32,128]{2,1,0:T(8,128)} %d_hbm.1), custom_call_target="tpu_custom_call" | custom-call | tf_op jit(solution)/shard_map/pallas_call | solution.py:494
  42.7 0.7 %copy.5 = f32[16,32,128]{2,1,0:T(8,128)} copy(f32[16,32,128]{2,1,0:T(8,128)S(1)} %shard_map.37) | data formatting | bytes 524288

commit v3 on v2

--- a/solution.py
+++ b/solution.py
@@ -114,6 +114,20 @@
     return total + w[4] * roll_z(value, group) + w[5] * roll_z(value, -group)
 
 
+class Halo:
+    def __init__(self, copy, sends, receives):
+        self.copy, self.sends, self.receives = copy, sends, receives
+
+    def start(self):
+        pl.when(self.sends)(self.copy.start)
+
+    def wait_send(self):
+        pl.when(self.sends)(self.copy.wait_send)
+
+    def wait_recv(self):
+        pl.when(self.receives)(self.copy.wait_recv)
+
+
 def kernel(
     sizes, p_hbm, s_hbm, d_hbm, o_hbm,
     p, d, s, v1, v2, fh, out, w0, g0, dg0,
@@ -124,13 +138,47 @@
     ib, iy = lax.axis_index("blk"), lax.axis_index("sub")
 
     def peer(dx, dy):
-        return {"blk": lax.rem(ib + (dx + n_blk), n_blk), "sub": lax.rem(iy + (dy + n_sub), n_sub)}
+        return {"blk": ib + dx, "sub": iy + dy}
+
+    def there(dx, dy):
+        known = []
+        if dx:
+            known.append(ib >= -dx if dx < 0 else ib < n_blk - dx)
+        if dy:
+            known.append(iy >= -dy if dy < 0 else iy < n_sub - dy)
+        return functools.reduce(jnp.logical_and, known)
 
     def remote(src, dst, sem, k, dx, dy):
-        return pltpu.make_async_remote_copy(
-            src_ref=src, dst_ref=dst, send_sem=sem.at[0, k], recv_sem=sem.at[1, k],
-            device_id=peer(dx, dy), device_id_type=MESH,
+        return Halo(
+            pltpu.make_async_remote_copy(
+                src_ref=src, dst_ref=dst, send_sem=sem.at[0, k], recv_sem=sem.at[1, k],
+                device_id=peer(dx, dy), device_id_type=MESH,
+            ),
+            there(dx, dy),
+            there(-dx, -dy),
         )
+
+    def clear_outside(ref, lead, x_side, x_count, rows, low_rows, high_rows):
+        planes = x_count + 2 * x_side
+        slab = jnp.zeros(lead + (x_side, rows, 128), jnp.float32)
+        strip = jnp.zeros(lead + (planes, low_rows[1], 128), jnp.float32)
+        every = (slice(None),) * len(lead)
+
+        @pl.when(ib == 0)
+        def _():
+            ref[every + (slice(0, x_side),)] = slab
+
+        @pl.when(ib == n_blk - 1)
+        def _():
+            ref[every + (slice(x_side + x_count, planes),)] = slab
+
+        @pl.when(iy == 0)
+        def _():
+            ref[every + (slice(None), slice(low_rows[0], low_rows[0] + low_rows[1]))] = strip
+
+        @pl.when(iy == n_sub - 1)
+        def _():
+            ref[every + (slice(None), slice(high_rows[0], high_rows[0] + high_rows[1]))] = strip
 
     local = [
         pltpu.make_async_copy(src, dst.at[pl.ds(3, 16), pl.ds(0, 32)], local_sem.at[k])
@@ -140,10 +188,31 @@
         copy.start()
     barrier = pltpu.get_barrier_semaphore()
     for dx, dy in DIRS:
-        pl.semaphore_signal(barrier, inc=1, device_id=peer(dx, dy), device_id_type=MESH)
+        @pl.when(there(dx, dy))
+        def _():
+            pl.semaphore_signal(barrier, inc=1, device_id=peer(dx, dy), device_id_type=MESH)
+
+    for ref in (d, p, s, fh):
+        clear_outside(ref, (), 3, 16, 40, (36, 4), (32, 4))
+    clear_outside(l1, (4,), 2, 4, 24, (20, 4), (16, 4))
+    clear_outside(b1, (), 2, 4, 24, (20, 4), (16, 4))
+    for index in (0, 1, 3, 4):
+        @pl.when((ib + (index - 2) < 0) | (ib + (index - 2) >= n_blk))
+        def _():
+            c2[:, index] = jnp.zeros((4, 24, 128), jnp.float32)
+            b2[index] = jnp.zeros((24, 128), jnp.float32)
+
+    for edge, first in ((0, 0), (n_sub - 1, 16)):
+        @pl.when(iy == edge)
+        def _():
+            c2[:, :, first:first + 8] = jnp.zeros((4, 5, 8, 128), jnp.float32)
+            b2[:, first:first + 8] = jnp.zeros((5, 8, 128), jnp.float32)
+
     for copy in local:
         copy.wait()
-    pl.semaphore_wait(barrier, len(DIRS))
+    across = 1 + (ib > 0).astype(jnp.int32) + (ib < n_blk - 1).astype(jnp.int32)
+    along = 1 + (iy > 0).astype(jnp.int32) + (iy < n_sub - 1).astype(jnp.int32)
+    pl.semaphore_wait(barrier, across * along - 1)
 
     def fine_copies(src, dst, sem, width):
         return [
@@ -161,29 +230,8 @@
     for copy in d_copies + p_copies + s_copies:
         copy.start()
 
-    def clear_fine(ref):
-        zero = jnp.zeros((3, 40, 128), jnp.float32)
-        strip = jnp.zeros((22, 4, 128), jnp.float32)
-
-        @pl.when(ib == 0)
-        def _():
-            ref[0:3] = zero
-
-        @pl.when(ib == n_blk - 1)
-        def _():
-            ref[19:22] = zero
-
-        @pl.when(iy == 0)
-        def _():
-            ref[:, 36:40] = strip
-
-        @pl.when(iy == n_sub - 1)
-        def _():
-            ref[:, 32:36] = strip
-
     for copy in d_copies:
         copy.wait_recv()
-    clear_fine(d)
 
     def x_face(i, _):
         xs[i] = d[2 * i + 2, 0:32] + d[2 * i + 3, 0:32]
@@ -294,7 +342,6 @@
 
     for copy in p_copies + s_copies:
         copy.wait_recv()
-    clear_fine(p)
 
     def scale_source(i, _):
         g0[i] = g0[i] * s[i]
@@ -346,25 +393,6 @@
 
     for copy in l1_copies:
         copy.wait_recv()
-    pairs = jnp.zeros((2, 24, 128), jnp.float32)
-    strip1 = jnp.zeros((8, 4, 128), jnp.float32)
-
-    @pl.when(ib == 0)
-    def _():
-        l1[3, 0:2] = pairs
-
-    @pl.when(ib == n_blk - 1)
-    def _():
-        l1[3, 6:8] = pairs
-
-    @pl.when(iy == 0)
-    def _():
-        l1[3, :, 20:24] = strip1
-
-    @pl.when(iy == n_sub - 1)
-    def _():
-        l1[3, :, 16:20] = strip1
-
     inv1 = l1[3]
     coarse_weights(w1, l1, inv1, 2, 0.25)
 
@@ -389,22 +417,6 @@
         copy.start()
     for copy in c2_copies:
         copy.wait_recv()
-    group = jnp.zeros((24, 128), jnp.float32)
-    strip2 = jnp.zeros((5, 8, 128), jnp.float32)
-
-    for index in range(5):
-        @pl.when((ib + (index - 2) < 0) | (ib + (index - 2) >= n_blk))
-        def _():
-            c2[3, index] = group
-
-    @pl.when(iy == 0)
-    def _():
-        c2[3, :, 0:8] = strip2
-
-    @pl.when(iy == n_sub - 1)
-    def _():
-        c2[3, :, 16:24] = strip2
-
     inv2 = c2[3]
     coarse_weights(w2, c2, inv2, 4, 0.0625)
 
@@ -447,7 +459,6 @@
 
     for copy in f_copies:
         copy.wait_recv()
-    clear_fine(fh)
 
     def correct(i, _):
         halves = (2 * i + 1, 2 * i + 2)

time: 43.6 us -> 32.5 us (0.75)
  Pallas kernels: 42.7 us -> 31.7 us
    pallas_call x1, Pallas kernels: 42.7 us -> 31.7 us  [on_device(): pl.pallas_call(functools.partial(kernel, sizes), out_shape=jax.ShapeDtype...]
where the time goes in v3:
time: 32.5 us; the launch traced here: 32.4 us
  Pallas kernels  31.7 us (98%)
  local copies, waits for them, and re-layouts  0.71 us (2%)
    pallas_call x1, Pallas kernels, on_device(): pl.pallas_call(functools.partial(kernel, sizes), out_shape=jax.ShapeDtype...  31.7 us
    unnamed x1, local copies, waits for them, and re-layouts  0.71 us

profile of v3, /device:TPU:1, one launch (start us, length us, event | category | flops | bytes accessed | tf_op | source)
XLA Modules:
  0.0 32.4 jit_solution(17681407387849197979)
XLA Ops:
  0.0 31.7 %shard_map.37 = f32[16,32,128]{2,1,0:T(8,128)S(1)} custom-call(f32[16,32,128]{2,1,0:T(8,128)} %p_hbm.1, f32[16,32,128]{2,1,0:T(8,128)} %s_hbm.1, f32[16,32,128]{2,1,0:T(8,128)} %d_hbm.1), custom_call_target="tpu_custom_call" | custom-call | tf_op jit(solution)/shard_map/pallas_call | solution.py:505
  31.7 0.7 %copy.5 = f32[16,32,128]{2,1,0:T(8,128)} copy(f32[16,32,128]{2,1,0:T(8,128)S(1)} %shard_map.37) | data formatting | bytes 524288

commit v4 on v3

--- a/solution.py
+++ b/solution.py
@@ -109,9 +109,13 @@
 
 
 def coarse_sum(w, value, group):
-    total = w[0] * x_down(value, behind(value), group) + w[1] * x_up(value, ahead(value), group)
-    total = total + w[2] * roll_y(value, 1) + w[3] * roll_y(value, -1)
-    return total + w[4] * roll_z(value, group) + w[5] * roll_z(value, -group)
+    return weighted_sum(w, value, behind(value), ahead(value), group)
+
+
+def weighted_sum(w, value, previous, following, group):
+    across = w[0] * x_down(value, previous, group) + w[1] * x_up(value, following, group)
+    along = w[2] * roll_y(value, 1) + w[3] * roll_y(value, -1)
+    return (along + (w[4] * roll_z(value, group) + w[5] * roll_z(value, -group))) + across
 
 
 class Halo:
@@ -130,7 +134,7 @@
 
 def kernel(
     sizes, p_hbm, s_hbm, d_hbm, o_hbm,
-    p, d, s, v1, v2, fh, out, w0, g0, dg0,
+    p, d, s, sx, v1, v2, fh, out, w0, g0, dg0,
     xs, ys, cs, l1, w1, b1, dg1, c2, w2, b2, e1, e0,
     local_sem, d_sem, p_sem, s_sem, f_sem, l1_sem, b1_sem, c2_sem, b2_sem,
 ):
@@ -180,18 +184,18 @@
         def _():
             ref[every + (slice(None), slice(high_rows[0], high_rows[0] + high_rows[1]))] = strip
 
+    barrier = pltpu.get_barrier_semaphore()
+    for dx, dy in DIRS:
+        @pl.when(there(dx, dy))
+        def _():
+            pl.semaphore_signal(barrier, inc=1, device_id=peer(dx, dy), device_id_type=MESH)
+
     local = [
         pltpu.make_async_copy(src, dst.at[pl.ds(3, 16), pl.ds(0, 32)], local_sem.at[k])
         for k, (src, dst) in enumerate(((d_hbm, d), (p_hbm, p), (s_hbm, s)))
     ]
     for copy in local:
         copy.start()
-    barrier = pltpu.get_barrier_semaphore()
-    for dx, dy in DIRS:
-        @pl.when(there(dx, dy))
-        def _():
-            pl.semaphore_signal(barrier, inc=1, device_id=peer(dx, dy), device_id_type=MESH)
-
     for ref in (d, p, s, fh):
         clear_outside(ref, (), 3, 16, 40, (36, 4), (32, 4))
     clear_outside(l1, (4,), 2, 4, 24, (20, 4), (16, 4))
@@ -210,23 +214,36 @@
 
     for copy in local:
         copy.wait()
+    def joined(plane, beyond):
+        face = 0.5 * (d[plane, 0:32] + d[beyond, 0:32])
+        return s[plane, 0:32] + face * p[beyond, 0:32]
+
+    sx[0, 0] = s[3, 0:32]
+    sx[0, 1] = joined(4, 5)
+    sx[1, 0] = joined(17, 16)
+    sx[1, 1] = s[18, 0:32]
+    p[0] = jnp.zeros((40, 128), jnp.float32)
+    p[21] = jnp.zeros((40, 128), jnp.float32)
+
     across = 1 + (ib > 0).astype(jnp.int32) + (ib < n_blk - 1).astype(jnp.int32)
     along = 1 + (iy > 0).astype(jnp.int32) + (iy < n_sub - 1).astype(jnp.int32)
     pl.semaphore_wait(barrier, across * along - 1)
 
-    def fine_copies(src, dst, sem, width):
-        return [
-            remote(
-                src.at[send_range(dx, 3, 16, width - abs(dy)), send_range(dy, 0, 32, 4)],
-                dst.at[planes_to(dx, 3, 16, width - abs(dy)), rows_to(dy, 32, 4)],
-                sem, k, dx, dy,
-            )
-            for k, (dx, dy) in enumerate(DIRS)
-        ]
+    def fine_copies(src, dst, sem, width, sides=None):
+        copies = []
+        for k, (dx, dy) in enumerate(DIRS):
+            count = min(width - abs(dy), 2) if src is p else width - abs(dy)
+            if sides is not None and dy == 0:
+                block = sides.at[0 if dx < 0 else 1]
+            else:
+                block = src.at[send_range(dx, 3, 16, count), send_range(dy, 0, 32, 4)]
+            target = dst.at[planes_to(dx, 3, 16, count), rows_to(dy, 32, 4)]
+            copies.append(remote(block, target, sem, k, dx, dy))
+        return copies
 
     d_copies = fine_copies(d, d, d_sem, 3)
     p_copies = fine_copies(p, p, p_sem, 3)
-    s_copies = fine_copies(s, s, s_sem, 2)
+    s_copies = fine_copies(s, s, s_sem, 2, sx)
     for copy in d_copies + p_copies + s_copies:
         copy.start()
 
@@ -339,6 +356,8 @@
         return here, above
 
     lax.fori_loop(1, 21, fine_weights, (d[0], d[1]), unroll=True)
+    w0[0, 1] = zero0
+    w0[1, 20] = zero0
 
     for copy in p_copies + s_copies:
         copy.wait_recv()
@@ -396,12 +415,14 @@
     inv1 = l1[3]
     coarse_weights(w1, l1, inv1, 2, 0.25)
 
+    for copy in d_copies + p_copies + s_copies:
+        copy.wait_send()
     for copy in b1_copies:
         copy.wait_recv()
     g1 = l1[3] * b1[...]
     err1 = g1
-    err1 = g1 + coarse_sum(w1, err1, 2) + KEEP * err1
-    res1 = (g1 + coarse_sum(w1, err1, 2) - WEIGHT * err1)[2:6, 0:16] * dg1[...]
+    err1 = (g1 + KEEP * err1) + coarse_sum(w1, err1, 2)
+    res1 = ((g1 - WEIGHT * err1) + coarse_sum(w1, err1, 2))[2:6, 0:16] * dg1[...]
     xs[0:4, 0:16] = res1
     b2[2, 8:16] = 0.125 * pack_groups(
         xs[0:4, pl.ds(0, 8, stride=2), :] + xs[0:4, pl.ds(1, 8, stride=2), :]
@@ -420,12 +441,20 @@
     inv2 = c2[3]
     coarse_weights(w2, c2, inv2, 4, 0.0625)
 
+    for copy in l1_copies + c2_copies + b1_copies:
+        copy.wait_send()
     for copy in b2_copies:
         copy.wait_recv()
     g2 = c2[3] * b2[...]
     err2 = g2
-    for _ in range(COARSE_SWEEPS):
-        err2 = g2 + coarse_sum(w2, err2, 4) + KEEP * err2
+    for _ in range(COARSE_SWEEPS - 3):
+        err2 = (g2 + KEEP * err2) + coarse_sum(w2, err2, 4)
+    w2_middle = [w2[k, 1:4] for k in range(6)]
+    g2 = g2[1:4]
+    total = weighted_sum(w2_middle, err2[1:4], err2[0:3], err2[2:5], 4)
+    err2 = (g2 + KEEP * err2[1:4]) + total
+    for _ in range(2):
+        err2 = (g2 + KEEP * err2) + coarse_sum(w2_middle, err2, 4)
 
     row = lax.broadcasted_iota(jnp.int32, (8, 128), 0)
 
@@ -436,13 +465,13 @@
             e1[pair, pl.ds(parity, 8, stride=2), :] = centre
             e1[pair, pl.ds(16 + parity, 8, stride=2), :] = sides
 
-    before, centre, after = spread_groups(err2[1]), spread_groups(err2[2]), spread_groups(err2[3])
+    before, centre, after = spread_groups(err2[0]), spread_groups(err2[1]), spread_groups(err2[2])
     for pair, value in enumerate(before[2:4] + centre + after[0:2]):
         put(pair, value)
     g1 = l1[3] * b1[...]
     err1 = err1 + e1[:, 0:24]
     for _ in range(POST):
-        err1 = g1 + coarse_sum(w1, err1, 2) + KEEP * err1
+        err1 = (g1 + KEEP * err1) + coarse_sum(w1, err1, 2)
 
     def put_fine(index, value):
         sides = jnp.where(row < 2, value[16:24], roll_y(value[16:24], 4))
@@ -457,6 +486,8 @@
         if pair < 6:
             put_fine(2 * pair - 2, odd_cell)
 
+    for copy in f_copies + b2_copies:
+        copy.wait_send()
     for copy in f_copies:
         copy.wait_recv()
 
@@ -488,8 +519,6 @@
         part = pl.ds(4 * k, 4)
         stores.append(pltpu.make_async_copy(out.at[part], o_hbm.at[part], local_sem.at[3 + k]))
         stores[-1].start()
-    for copy in d_copies + p_copies + s_copies + l1_copies + c2_copies + f_copies + b1_copies + b2_copies:
-        copy.wait_send()
     for store in stores:
         store.wait()
 
@@ -508,7 +537,7 @@
             in_specs=[pl.BlockSpec(memory_space=pltpu.HBM)] * 3,
             out_specs=pl.BlockSpec(memory_space=pl.ANY),
             scratch_shapes=[
-                vmem(22, 40, 128), vmem(22, 40, 128), vmem(22, 40, 128),
+                vmem(22, 40, 128), vmem(22, 40, 128), vmem(22, 40, 128), vmem(2, 2, 32, 128),
                 vmem(22, 40, 128), vmem(22, 40, 128), vmem(22, 40, 128),
                 vmem(16, 32, 128), vmem(6, 22, 40, 128), vmem(22, 40, 128), vmem(22, 40, 128),
                 vmem(10, 32, 128), vmem(8, 48, 128), vmem(6, 4, 16, 128),

time: 32.5 us -> 31.9 us (0.982)
  Pallas kernels: 31.7 us -> 31 us
    pallas_call x1, Pallas kernels: 31.7 us -> 31 us  [on_device(): pl.pallas_call(functools.partial(kernel, sizes), out_shape=jax.ShapeDtype...]
where the time goes in v4:
time: 31.9 us; the launch traced here: 31.8 us
  Pallas kernels  31 us (97%)
  local copies, waits for them, and re-layouts  0.71 us (2%)
    pallas_call x1, Pallas kernels, on_device(): pl.pallas_call(functools.partial(kernel, sizes), out_shape=jax.ShapeDtype...  31 us
    unnamed x1, local copies, waits for them, and re-layouts  0.71 us

profile of v4, /device:TPU:1, one launch (start us, length us, event | category | flops | bytes accessed | tf_op | source)
XLA Modules:
  0.0 31.8 jit_solution(3616307630204329453)
XLA Ops:
  0.0 31.0 %shard_map.37 = f32[16,32,128]{2,1,0:T(8,128)S(1)} custom-call(f32[16,32,128]{2,1,0:T(8,128)} %p_hbm.1, f32[16,32,128]{2,1,0:T(8,128)} %s_hbm.1, f32[16,32,128]{2,1,0:T(8,128)} %d_hbm.1), custom_call_target="tpu_custom_call" | custom-call | tf_op jit(solution)/shard_map/pallas_call | solution.py:534
  31.1 0.7 %copy.5 = f32[16,32,128]{2,1,0:T(8,128)} copy(f32[16,32,128]{2,1,0:T(8,128)S(1)} %shard_map.37) | data formatting | bytes 524288

commit v5 on v4

--- a/solution.py
+++ b/solution.py
@@ -121,9 +121,10 @@
 class Halo:
     def __init__(self, copy, sends, receives):
         self.copy, self.sends, self.receives = copy, sends, receives
+        self.starts = sends
 
     def start(self):
-        pl.when(self.sends)(self.copy.start)
+        pl.when(self.starts)(self.copy.start)
 
     def wait_send(self):
         pl.when(self.sends)(self.copy.wait_send)
@@ -134,9 +135,9 @@
 
 def kernel(
     sizes, p_hbm, s_hbm, d_hbm, o_hbm,
-    p, d, s, sx, v1, v2, fh, out, w0, g0, dg0,
+    p, d, s, sx, p_mate, d_mate, s_mate, v1, v2, fh, out, w0, g0, dg0,
     xs, ys, cs, l1, w1, b1, dg1, c2, w2, b2, e1, e0,
-    local_sem, d_sem, p_sem, s_sem, f_sem, l1_sem, b1_sem, c2_sem, b2_sem,
+    local_sem, d_mate_sem, p_mate_sem, s_mate_sem, d_sem, p_sem, s_sem, f_sem, l1_sem, b1_sem, c2_sem, b2_sem,
 ):
     n_blk, n_sub = sizes
     ib, iy = lax.axis_index("blk"), lax.axis_index("sub")
@@ -184,11 +185,16 @@
         def _():
             ref[every + (slice(None), slice(high_rows[0], high_rows[0] + high_rows[1]))] = strip
 
+    odd_one = lax.rem(iy, 2) == 1
+    even_one = jnp.logical_not(odd_one)
     barrier = pltpu.get_barrier_semaphore()
-    for dx, dy in DIRS:
-        @pl.when(there(dx, dy))
-        def _():
-            pl.semaphore_signal(barrier, inc=1, device_id=peer(dx, dy), device_id_type=MESH)
+
+    def announce(dx, dy):
+        pl.semaphore_signal(barrier, inc=1, device_id=peer(dx, dy), device_id_type=MESH)
+
+    pl.when(even_one)(functools.partial(announce, 0, 1))
+    for dx, dy in [(i, j) for j in (-2, 1, 0, -1) for i in (-1, 1, 0) if (i, j) != (0, 0)]:
+        pl.when(odd_one & there(dx, dy))(functools.partial(announce, dx, dy))
 
     local = [
         pltpu.make_async_copy(src, dst.at[pl.ds(3, 16), pl.ds(0, 32)], local_sem.at[k])
@@ -226,26 +232,65 @@
     p[21] = jnp.zeros((40, 128), jnp.float32)
 
     across = 1 + (ib > 0).astype(jnp.int32) + (ib < n_blk - 1).astype(jnp.int32)
-    along = 1 + (iy > 0).astype(jnp.int32) + (iy < n_sub - 1).astype(jnp.int32)
-    pl.semaphore_wait(barrier, across * along - 1)
-
-    def fine_copies(src, dst, sem, width, sides=None):
+    behind_me = (iy > 0).astype(jnp.int32)
+    beyond_mate = (iy + 2 < n_sub).astype(jnp.int32)
+    pl.semaphore_wait(barrier, across * jnp.where(odd_one, 1 + beyond_mate, 1 + behind_me))
+
+    def slices(dx, dy, width):
+        return (
+            (send_range(dx, 3, 16, width), send_range(dy, 0, 32, 4)),
+            (planes_to(dx, 3, 16, width), rows_to(dy, 32, 4)),
+        )
+
+    def fine_copies(src, dst, sem, width):
         copies = []
         for k, (dx, dy) in enumerate(DIRS):
-            count = min(width - abs(dy), 2) if src is p else width - abs(dy)
-            if sides is not None and dy == 0:
-                block = sides.at[0 if dx < 0 else 1]
-            else:
-                block = src.at[send_range(dx, 3, 16, count), send_range(dy, 0, 32, 4)]
-            target = dst.at[planes_to(dx, 3, 16, count), rows_to(dy, 32, 4)]
-            copies.append(remote(block, target, sem, k, dx, dy))
+            here, target = slices(dx, dy, width - abs(dy))
+            copies.append(remote(src.at[here], dst.at[target], sem, k, dx, dy))
         return copies
 
-    d_copies = fine_copies(d, d, d_sem, 3)
-    p_copies = fine_copies(p, p, p_sem, 3)
-    s_copies = fine_copies(s, s, s_sem, 2, sx)
-    for copy in d_copies + p_copies + s_copies:
-        copy.start()
+    def first_copies(ref, mate, sem, mate_sem, width, side_width, sides=None):
+        copies, through, onward = [], [], []
+        for k, (dx, dy) in enumerate(DIRS):
+            here, target = slices(dx, dy, min(width - abs(dy), side_width) if dx else width)
+            block = ref.at[here] if sides is None or dy else sides.at[0 if dx < 0 else 1]
+            copies.append(remote(block, ref.at[target], sem, k, dx, dy))
+            if (dx, dy) == (0, -1):
+                continue
+            target_even = odd_one if dy else even_one
+            copies[-1].starts = there(dx, dy) & jnp.logical_not(target_even)
+            copy = pltpu.make_async_remote_copy(
+                src_ref=block, dst_ref=mate.at[target], send_sem=sem.at[0, k],
+                recv_sem=mate_sem.at[0, k], device_id=peer(dx, dy + 1), device_id_type=MESH,
+            )
+            from_x = ib >= dx if dx > 0 else ib < n_blk + dx
+            from_y = iy >= 1 + dy if dy >= 0 else iy < n_sub + 1 + dy
+            through.append(Halo(copy, there(dx, dy) & target_even, odd_one & from_x & from_y))
+            copy = pltpu.make_async_remote_copy(
+                src_ref=mate.at[target], dst_ref=ref.at[target], send_sem=mate_sem.at[1, k],
+                recv_sem=sem.at[1, k], device_id=peer(0, -1), device_id_type=MESH,
+            )
+            onward.append(Halo(copy, through[-1].receives, None))
+        return copies, through, onward
+
+    def hand_on(through, onward):
+        for arriving, leaving in zip(through, onward):
+            @pl.when(arriving.receives)
+            def _():
+                arriving.copy.wait_recv()
+                leaving.copy.start()
+
+    d_copies, d_through, d_onward = first_copies(d, d_mate, d_sem, d_mate_sem, 3, 3)
+    p_copies, p_through, p_onward = first_copies(p, p_mate, p_sem, p_mate_sem, 3, 2)
+    s_copies, s_through, s_onward = first_copies(s, s_mate, s_sem, s_mate_sem, 2, 2, sx)
+    for copies, through in ((d_copies, d_through), (p_copies, p_through), (s_copies, s_through)):
+        for k, copy in enumerate(copies):
+            copy.start()
+            if k < 6:
+                through[k].start()
+            elif k == 7:
+                through[6].start()
+    hand_on(d_through, d_onward)
 
     for copy in d_copies:
         copy.wait_recv()
@@ -304,6 +349,8 @@
     ]
     for copy in l1_copies:
         copy.start()
+    hand_on(p_through, p_onward)
+    hand_on(s_through, s_onward)
 
     for k, face in enumerate((lx, ux, ly, uy, lz, uz)):
         cs[k] = face
@@ -407,15 +454,17 @@
         for k, (dx, dy) in enumerate(DIRS)
     ]
     f_copies = fine_copies(v2, fh, f_sem, 2)
-    for copy in b1_copies + c2_copies:
+    for copy in b1_copies:
         copy.start()
 
     for copy in l1_copies:
         copy.wait_recv()
+    for copy in c2_copies:
+        copy.start()
     inv1 = l1[3]
     coarse_weights(w1, l1, inv1, 2, 0.25)
 
-    for copy in d_copies + p_copies + s_copies:
+    for copy in d_copies + p_copies + s_copies + d_onward + p_onward + s_onward:
         copy.wait_send()
     for copy in b1_copies:
         copy.wait_recv()
@@ -539,12 +588,14 @@
             scratch_shapes=[
                 vmem(22, 40, 128), vmem(22, 40, 128), vmem(22, 40, 128), vmem(2, 2, 32, 128),
                 vmem(22, 40, 128), vmem(22, 40, 128), vmem(22, 40, 128),
+                vmem(22, 40, 128), vmem(22, 40, 128), vmem(22, 40, 128),
                 vmem(16, 32, 128), vmem(6, 22, 40, 128), vmem(22, 40, 128), vmem(22, 40, 128),
                 vmem(10, 32, 128), vmem(8, 48, 128), vmem(6, 4, 16, 128),
                 vmem(4, 8, 24, 128), vmem(6, 8, 24, 128), vmem(8, 24, 128), vmem(4, 16, 128),
                 vmem(4, 5, 24, 128), vmem(6, 5, 24, 128), vmem(5, 24, 128),
                 vmem(8, 32, 128), vmem(10, 48, 128),
                 pltpu.SemaphoreType.DMA((7,)),
+                pltpu.SemaphoreType.DMA((2, near)), pltpu.SemaphoreType.DMA((2, near)), pltpu.SemaphoreType.DMA((2, near)),
                 pltpu.SemaphoreType.DMA((2, near)), pltpu.SemaphoreType.DMA((2, near)),
                 pltpu.SemaphoreType.DMA((2, near)), pltpu.SemaphoreType.DMA((2, near)),
                 pltpu.SemaphoreType.DMA((2, near)), pltpu.SemaphoreType.DMA((2, near)),

time: 31.9 us -> 33.7 us (1.056)
  Pallas kernels: 31 us -> 32.8 us
    pallas_call x1, Pallas kernels: 31 us -> 32.8 us  [on_device(): pl.pallas_call(functools.partial(kernel, sizes), out_shape=jax.ShapeDtype...]
where the time goes in v5:
time: 33.7 us; the launch traced here: 33.5 us
  Pallas kernels  32.8 us (97%)
  local copies, waits for them, and re-layouts  0.71 us (2%)
    pallas_call x1, Pallas kernels, on_device(): pl.pallas_call(functools.partial(kernel, sizes), out_shape=jax.ShapeDtype...  32.8 us
    unnamed x1, local copies, waits for them, and re-layouts  0.71 us

profile of v5, /device:TPU:1, one launch (start us, length us, event | category | flops | bytes accessed | tf_op | source)
XLA Modules:
  0.0 33.5 jit_solution(10859233206733873121)
XLA Ops:
  0.0 32.8 %shard_map.37 = f32[16,32,128]{2,1,0:T(8,128)S(1)} custom-call(f32[16,32,128]{2,1,0:T(8,128)} %p_hbm.1, f32[16,32,128]{2,1,0:T(8,128)} %s_hbm.1, f32[16,32,128]{2,1,0:T(8,128)} %d_hbm.1), custom_call_target="tpu_custom_call" | custom-call | tf_op jit(solution)/shard_map/pallas_call | solution.py:583
  32.8 0.7 %copy.5 = f32[16,32,128]{2,1,0:T(8,128)} copy(f32[16,32,128]{2,1,0:T(8,128)S(1)} %shard_map.37) | data formatting | bytes 524288

commit v6 on v4

--- a/solution.py
+++ b/solution.py
@@ -121,9 +121,10 @@
 class Halo:
     def __init__(self, copy, sends, receives):
         self.copy, self.sends, self.receives = copy, sends, receives
+        self.starts = sends
 
     def start(self):
-        pl.when(self.sends)(self.copy.start)
+        pl.when(self.starts)(self.copy.start)
 
     def wait_send(self):
         pl.when(self.sends)(self.copy.wait_send)
@@ -134,9 +135,9 @@
 
 def kernel(
     sizes, p_hbm, s_hbm, d_hbm, o_hbm,
-    p, d, s, sx, v1, v2, fh, out, w0, g0, dg0,
+    p, d, s, sx, p_mate, d_mate, s_mate, v1, v2, fh, out, w0, g0, dg0,
     xs, ys, cs, l1, w1, b1, dg1, c2, w2, b2, e1, e0,
-    local_sem, d_sem, p_sem, s_sem, f_sem, l1_sem, b1_sem, c2_sem, b2_sem,
+    local_sem, d_mate_sem, p_mate_sem, s_mate_sem, d_sem, p_sem, s_sem, f_sem, l1_sem, b1_sem, c2_sem, b2_sem,
 ):
     n_blk, n_sub = sizes
     ib, iy = lax.axis_index("blk"), lax.axis_index("sub")
@@ -184,11 +185,16 @@
         def _():
             ref[every + (slice(None), slice(high_rows[0], high_rows[0] + high_rows[1]))] = strip
 
+    odd_one = lax.rem(iy, 2) == 1
+    even_one = jnp.logical_not(odd_one)
     barrier = pltpu.get_barrier_semaphore()
-    for dx, dy in DIRS:
-        @pl.when(there(dx, dy))
-        def _():
-            pl.semaphore_signal(barrier, inc=1, device_id=peer(dx, dy), device_id_type=MESH)
+
+    def announce(dx, dy):
+        pl.semaphore_signal(barrier, inc=1, device_id=peer(dx, dy), device_id_type=MESH)
+
+    pl.when(even_one)(functools.partial(announce, 0, 1))
+    for dx, dy in [(i, j) for j in (-2, 1, 0, -1) for i in (-1, 1, 0) if (i, j) != (0, 0)]:
+        pl.when(odd_one & there(dx, dy))(functools.partial(announce, dx, dy))
 
     local = [
         pltpu.make_async_copy(src, dst.at[pl.ds(3, 16), pl.ds(0, 32)], local_sem.at[k])
@@ -196,6 +202,70 @@
     ]
     for copy in local:
         copy.start()
+    across = 1 + (ib > 0).astype(jnp.int32) + (ib < n_blk - 1).astype(jnp.int32)
+    behind_me = (iy > 0).astype(jnp.int32)
+    beyond_mate = (iy + 2 < n_sub).astype(jnp.int32)
+    pl.semaphore_wait(barrier, across * jnp.where(odd_one, 1 + beyond_mate, 1 + behind_me))
+
+    def slices(dx, dy, width):
+        return (
+            (send_range(dx, 3, 16, width), send_range(dy, 0, 32, 4)),
+            (planes_to(dx, 3, 16, width), rows_to(dy, 32, 4)),
+        )
+
+    def fine_copies(src, dst, sem, width):
+        copies = []
+        for k, (dx, dy) in enumerate(DIRS):
+            here, target = slices(dx, dy, width - abs(dy))
+            copies.append(remote(src.at[here], dst.at[target], sem, k, dx, dy))
+        return copies
+
+    def first_copies(ref, hbm, mate, sem, mate_sem, width, side_width, sides=None):
+        copies, through, onward = [], [], []
+        for k, (dx, dy) in enumerate(DIRS):
+            here, target = slices(dx, dy, min(width - abs(dy), side_width) if dx else width)
+            block = hbm.at[pl.ds(here[0].start - 3, here[0].size), here[1]]
+            if sides is not None and dy == 0:
+                block = sides.at[0 if dx < 0 else 1]
+            copies.append(remote(block, ref.at[target], sem, k, dx, dy))
+            if (dx, dy) == (0, -1):
+                continue
+            target_even = odd_one if dy else even_one
+            copies[-1].starts = there(dx, dy) & jnp.logical_not(target_even)
+            copy = pltpu.make_async_remote_copy(
+                src_ref=block, dst_ref=mate.at[target], send_sem=sem.at[0, k],
+                recv_sem=mate_sem.at[0, k], device_id=peer(dx, dy + 1), device_id_type=MESH,
+            )
+            from_x = ib >= dx if dx > 0 else ib < n_blk + dx
+            from_y = iy >= 1 + dy if dy >= 0 else iy < n_sub + 1 + dy
+            through.append(Halo(copy, there(dx, dy) & target_even, odd_one & from_x & from_y))
+            copy = pltpu.make_async_remote_copy(
+                src_ref=mate.at[target], dst_ref=ref.at[target], send_sem=mate_sem.at[1, k],
+                recv_sem=sem.at[1, k], device_id=peer(0, -1), device_id_type=MESH,
+            )
+            onward.append(Halo(copy, through[-1].receives, None))
+        return copies, through, onward
+
+    def hand_on(through, onward):
+        for arriving, leaving in zip(through, onward):
+            @pl.when(arriving.receives)
+            def _():
+                arriving.copy.wait_recv()
+                leaving.copy.start()
+
+    d_copies, d_through, d_onward = first_copies(d, d_hbm, d_mate, d_sem, d_mate_sem, 3, 3)
+    p_copies, p_through, p_onward = first_copies(p, p_hbm, p_mate, p_sem, p_mate_sem, 3, 2)
+    s_copies, s_through, s_onward = first_copies(s, s_hbm, s_mate, s_sem, s_mate_sem, 2, 2, sx)
+    def send_first(copies, through):
+        for k, copy in enumerate(copies):
+            copy.start()
+            if k < 6:
+                through[k].start()
+            elif k == 7:
+                through[6].start()
+
+    send_first(d_copies, d_through)
+    send_first(p_copies, p_through)
     for ref in (d, p, s, fh):
         clear_outside(ref, (), 3, 16, 40, (36, 4), (32, 4))
     clear_outside(l1, (4,), 2, 4, 24, (20, 4), (16, 4))
@@ -225,27 +295,8 @@
     p[0] = jnp.zeros((40, 128), jnp.float32)
     p[21] = jnp.zeros((40, 128), jnp.float32)
 
-    across = 1 + (ib > 0).astype(jnp.int32) + (ib < n_blk - 1).astype(jnp.int32)
-    along = 1 + (iy > 0).astype(jnp.int32) + (iy < n_sub - 1).astype(jnp.int32)
-    pl.semaphore_wait(barrier, across * along - 1)
-
-    def fine_copies(src, dst, sem, width, sides=None):
-        copies = []
-        for k, (dx, dy) in enumerate(DIRS):
-            count = min(width - abs(dy), 2) if src is p else width - abs(dy)
-            if sides is not None and dy == 0:
-                block = sides.at[0 if dx < 0 else 1]
-            else:
-                block = src.at[send_range(dx, 3, 16, count), send_range(dy, 0, 32, 4)]
-            target = dst.at[planes_to(dx, 3, 16, count), rows_to(dy, 32, 4)]
-            copies.append(remote(block, target, sem, k, dx, dy))
-        return copies
-
-    d_copies = fine_copies(d, d, d_sem, 3)
-    p_copies = fine_copies(p, p, p_sem, 3)
-    s_copies = fine_copies(s, s, s_sem, 2, sx)
-    for copy in d_copies + p_copies + s_copies:
-        copy.start()
+    send_first(s_copies, s_through)
+    hand_on(d_through, d_onward)
 
     for copy in d_copies:
         copy.wait_recv()
@@ -304,6 +355,8 @@
     ]
     for copy in l1_copies:
         copy.start()
+    hand_on(p_through, p_onward)
+    hand_on(s_through, s_onward)
 
     for k, face in enumerate((lx, ux, ly, uy, lz, uz)):
         cs[k] = face
@@ -407,15 +460,17 @@
         for k, (dx, dy) in enumerate(DIRS)
     ]
     f_copies = fine_copies(v2, fh, f_sem, 2)
-    for copy in b1_copies + c2_copies:
+    for copy in b1_copies:
         copy.start()
 
     for copy in l1_copies:
         copy.wait_recv()
+    for copy in c2_copies:
+        copy.start()
     inv1 = l1[3]
     coarse_weights(w1, l1, inv1, 2, 0.25)
 
-    for copy in d_copies + p_copies + s_copies:
+    for copy in d_copies + p_copies + s_copies + d_onward + p_onward + s_onward:
         copy.wait_send()
     for copy in b1_copies:
         copy.wait_recv()
@@ -539,12 +594,14 @@
             scratch_shapes=[
                 vmem(22, 40, 128), vmem(22, 40, 128), vmem(22, 40, 128), vmem(2, 2, 32, 128),
                 vmem(22, 40, 128), vmem(22, 40, 128), vmem(22, 40, 128),
+                vmem(22, 40, 128), vmem(22, 40, 128), vmem(22, 40, 128),
                 vmem(16, 32, 128), vmem(6, 22, 40, 128), vmem(22, 40, 128), vmem(22, 40, 128),
                 vmem(10, 32, 128), vmem(8, 48, 128), vmem(6, 4, 16, 128),
                 vmem(4, 8, 24, 128), vmem(6, 8, 24, 128), vmem(8, 24, 128), vmem(4, 16, 128),
                 vmem(4, 5, 24, 128), vmem(6, 5, 24, 128), vmem(5, 24, 128),
                 vmem(8, 32, 128), vmem(10, 48, 128),
                 pltpu.SemaphoreType.DMA((7,)),
+                pltpu.SemaphoreType.DMA((2, near)), pltpu.SemaphoreType.DMA((2, near)), pltpu.SemaphoreType.DMA((2, near)),
                 pltpu.SemaphoreType.DMA((2, near)), pltpu.SemaphoreType.DMA((2, near)),
                 pltpu.SemaphoreType.DMA((2, near)), pltpu.SemaphoreType.DMA((2, near)),
                 pltpu.SemaphoreType.DMA((2, near)), pltpu.SemaphoreType.DMA((2, near)),

time: 31.9 us -> 33.7 us (1.056)
  Pallas kernels: 31 us -> 32.8 us
    pallas_call x1, Pallas kernels: 31 us -> 32.8 us  [on_device(): pl.pallas_call(functools.partial(kernel, sizes), out_shape=jax.ShapeDtype...]
where the time goes in v6:
time: 33.7 us; the launch traced here: 33.5 us
  Pallas kernels  32.8 us (97%)
  local copies, waits for them, and re-layouts  0.71 us (2%)
    pallas_call x1, Pallas kernels, on_device(): pl.pallas_call(functools.partial(kernel, sizes), out_shape=jax.ShapeDtype...  32.8 us
    unnamed x1, local copies, waits for them, and re-layouts  0.71 us

profile of v6, /device:TPU:1, one launch (start us, length us, event | category | flops | bytes accessed | tf_op | source)
XLA Modules:
  0.0 33.5 jit_solution(5020803427687948194)
XLA Ops:
  0.0 32.8 %shard_map.37 = f32[16,32,128]{2,1,0:T(8,128)S(1)} custom-call(f32[16,32,128]{2,1,0:T(8,128)} %p_hbm.1, f32[16,32,128]{2,1,0:T(8,128)} %s_hbm.1, f32[16,32,128]{2,1,0:T(8,128)} %d_hbm.1), custom_call_target="tpu_custom_call" | custom-call | tf_op jit(solution)/shard_map/pallas_call | solution.py:589
  32.8 0.7 %copy.5 = f32[16,32,128]{2,1,0:T(8,128)} copy(f32[16,32,128]{2,1,0:T(8,128)S(1)} %shard_map.37) | data formatting | bytes 524288

commit v7 on v4

--- a/solution.py
+++ b/solution.py
@@ -134,11 +134,12 @@
 
 def kernel(
     sizes, p_hbm, s_hbm, d_hbm, o_hbm,
-    p, d, s, sx, v1, v2, fh, out, w0, g0, dg0,
+    ps, d, sx, v1, v2, fh, out, w0, g0, dg0,
     xs, ys, cs, l1, w1, b1, dg1, c2, w2, b2, e1, e0,
-    local_sem, d_sem, p_sem, s_sem, f_sem, l1_sem, b1_sem, c2_sem, b2_sem,
+    local_sem, d_sem, ps_sem, f_sem, l1_sem, b1_sem, c2_sem, b2_sem,
 ):
     n_blk, n_sub = sizes
+    p, s = ps.at[0], ps.at[1]
     ib, iy = lax.axis_index("blk"), lax.axis_index("sub")
 
     def peer(dx, dy):
@@ -196,8 +197,9 @@
     ]
     for copy in local:
         copy.start()
-    for ref in (d, p, s, fh):
+    for ref in (d, fh):
         clear_outside(ref, (), 3, 16, 40, (36, 4), (32, 4))
+    clear_outside(ps, (2,), 3, 16, 40, (36, 4), (32, 4))
     clear_outside(l1, (4,), 2, 4, 24, (20, 4), (16, 4))
     clear_outside(b1, (), 2, 4, 24, (20, 4), (16, 4))
     for index in (0, 1, 3, 4):
@@ -218,10 +220,12 @@
         face = 0.5 * (d[plane, 0:32] + d[beyond, 0:32])
         return s[plane, 0:32] + face * p[beyond, 0:32]
 
-    sx[0, 0] = s[3, 0:32]
-    sx[0, 1] = joined(4, 5)
-    sx[1, 0] = joined(17, 16)
-    sx[1, 1] = s[18, 0:32]
+    sx[0, 0] = p[3:5, 0:32]
+    sx[0, 1, 0] = s[3, 0:32]
+    sx[0, 1, 1] = joined(4, 5)
+    sx[1, 0] = p[17:19, 0:32]
+    sx[1, 1, 0] = joined(17, 16)
+    sx[1, 1, 1] = s[18, 0:32]
     p[0] = jnp.zeros((40, 128), jnp.float32)
     p[21] = jnp.zeros((40, 128), jnp.float32)
 
@@ -229,22 +233,24 @@
     along = 1 + (iy > 0).astype(jnp.int32) + (iy < n_sub - 1).astype(jnp.int32)
     pl.semaphore_wait(barrier, across * along - 1)
 
-    def fine_copies(src, dst, sem, width, sides=None):
+    def fine_copies(src, dst, sem, width):
         copies = []
         for k, (dx, dy) in enumerate(DIRS):
-            count = min(width - abs(dy), 2) if src is p else width - abs(dy)
-            if sides is not None and dy == 0:
-                block = sides.at[0 if dx < 0 else 1]
-            else:
-                block = src.at[send_range(dx, 3, 16, count), send_range(dy, 0, 32, 4)]
+            count = width - abs(dy)
+            block = src.at[send_range(dx, 3, 16, count), send_range(dy, 0, 32, 4)]
             target = dst.at[planes_to(dx, 3, 16, count), rows_to(dy, 32, 4)]
             copies.append(remote(block, target, sem, k, dx, dy))
         return copies
 
     d_copies = fine_copies(d, d, d_sem, 3)
-    p_copies = fine_copies(p, p, p_sem, 3)
-    s_copies = fine_copies(s, s, s_sem, 2, sx)
-    for copy in d_copies + p_copies + s_copies:
+    ps_copies = []
+    for k, (dx, dy) in enumerate(DIRS):
+        block = ps.at[:, send_range(dx, 3, 16, 2), send_range(dy, 0, 32, 4)]
+        if dy == 0:
+            block = sx.at[0 if dx < 0 else 1]
+        target = ps.at[:, planes_to(dx, 3, 16, 2), rows_to(dy, 32, 4)]
+        ps_copies.append(remote(block, target, ps_sem, k, dx, dy))
+    for copy in d_copies + ps_copies:
         copy.start()
 
     for copy in d_copies:
@@ -359,7 +365,7 @@
     w0[0, 1] = zero0
     w0[1, 20] = zero0
 
-    for copy in p_copies + s_copies:
+    for copy in ps_copies:
         copy.wait_recv()
 
     def scale_source(i, _):
@@ -415,7 +421,7 @@
     inv1 = l1[3]
     coarse_weights(w1, l1, inv1, 2, 0.25)
 
-    for copy in d_copies + p_copies + s_copies:
+    for copy in d_copies + ps_copies:
         copy.wait_send()
     for copy in b1_copies:
         copy.wait_recv()
@@ -514,9 +520,9 @@
 
     carry = (fh[2], fh[3])
     stores = []
-    for k in range(4):
-        carry = lax.fori_loop(4 * k + 3, 4 * k + 7, last_sweep, carry, unroll=True)
-        part = pl.ds(4 * k, 4)
+    for k, (low, high) in enumerate(((0, 6), (6, 11), (11, 14), (14, 16))):
+        carry = lax.fori_loop(low + 3, high + 3, last_sweep, carry, unroll=True)
+        part = pl.ds(low, high - low)
         stores.append(pltpu.make_async_copy(out.at[part], o_hbm.at[part], local_sem.at[3 + k]))
         stores[-1].start()
     for store in stores:
@@ -537,7 +543,7 @@
             in_specs=[pl.BlockSpec(memory_space=pltpu.HBM)] * 3,
             out_specs=pl.BlockSpec(memory_space=pl.ANY),
             scratch_shapes=[
-                vmem(22, 40, 128), vmem(22, 40, 128), vmem(22, 40, 128), vmem(2, 2, 32, 128),
+                vmem(2, 22, 40, 128), vmem(22, 40, 128), vmem(2, 2, 2, 32, 128),
                 vmem(22, 40, 128), vmem(22, 40, 128), vmem(22, 40, 128),
                 vmem(16, 32, 128), vmem(6, 22, 40, 128), vmem(22, 40, 128), vmem(22, 40, 128),
                 vmem(10, 32, 128), vmem(8, 48, 128), vmem(6, 4, 16, 128),
@@ -547,7 +553,7 @@
                 pltpu.SemaphoreType.DMA((7,)),
                 pltpu.SemaphoreType.DMA((2, near)), pltpu.SemaphoreType.DMA((2, near)),
                 pltpu.SemaphoreType.DMA((2, near)), pltpu.SemaphoreType.DMA((2, near)),
-                pltpu.SemaphoreType.DMA((2, near)), pltpu.SemaphoreType.DMA((2, near)),
+                pltpu.SemaphoreType.DMA((2, near)),
                 pltpu.SemaphoreType.DMA((2, far)), pltpu.SemaphoreType.DMA((2, far)),
             ],
             compiler_params=pltpu.CompilerParams(

time: 31.9 us -> 32.1 us (level)
  no operation moved by 1% of the time
where the time goes in v7:
time: 32.1 us; the launch traced here: 31.9 us
  Pallas kernels  31.2 us (97%)
  local copies, waits for them, and re-layouts  0.71 us (2%)
    pallas_call x1, Pallas kernels, on_device(): pl.pallas_call(functools.partial(kernel, sizes), out_shape=jax.ShapeDtype...  31.2 us
    unnamed x1, local copies, waits for them, and re-layouts  0.71 us

profile of v7, /device:TPU:1, one launch (start us, length us, event | category | flops | bytes accessed | tf_op | source)
XLA Modules:
  0.0 31.9 jit_solution(28952893010379920)
XLA Ops:
  0.0 31.2 %shard_map.37 = f32[16,32,128]{2,1,0:T(8,128)S(1)} custom-call(f32[16,32,128]{2,1,0:T(8,128)} %p_hbm.1, f32[16,32,128]{2,1,0:T(8,128)} %s_hbm.1, f32[16,32,128]{2,1,0:T(8,128)} %d_hbm.1), custom_call_target="tpu_custom_call" | custom-call | tf_op jit(solution)/shard_map/pallas_call | solution.py:540
  31.2 0.7 %copy.5 = f32[16,32,128]{2,1,0:T(8,128)} copy(f32[16,32,128]{2,1,0:T(8,128)S(1)} %shard_map.37) | data formatting | bytes 524288

commit v8 on v7

--- a/solution.py
+++ b/solution.py
@@ -214,8 +214,26 @@
             c2[:, :, first:first + 8] = jnp.zeros((4, 5, 8, 128), jnp.float32)
             b2[:, first:first + 8] = jnp.zeros((5, 8, 128), jnp.float32)
 
-    for copy in local:
+    local[0].wait()
+    across = 1 + (ib > 0).astype(jnp.int32) + (ib < n_blk - 1).astype(jnp.int32)
+    along = 1 + (iy > 0).astype(jnp.int32) + (iy < n_sub - 1).astype(jnp.int32)
+    pl.semaphore_wait(barrier, across * along - 1)
+
+    def fine_copies(src, dst, sem, width):
+        copies = []
+        for k, (dx, dy) in enumerate(DIRS):
+            count = width - abs(dy)
+            block = src.at[send_range(dx, 3, 16, count), send_range(dy, 0, 32, 4)]
+            target = dst.at[planes_to(dx, 3, 16, count), rows_to(dy, 32, 4)]
+            copies.append(remote(block, target, sem, k, dx, dy))
+        return copies
+
+    d_copies = fine_copies(d, d, d_sem, 3)
+    for copy in d_copies:
+        copy.start()
+    for copy in local[1:]:
         copy.wait()
+
     def joined(plane, beyond):
         face = 0.5 * (d[plane, 0:32] + d[beyond, 0:32])
         return s[plane, 0:32] + face * p[beyond, 0:32]
@@ -229,20 +247,6 @@
     p[0] = jnp.zeros((40, 128), jnp.float32)
     p[21] = jnp.zeros((40, 128), jnp.float32)
 
-    across = 1 + (ib > 0).astype(jnp.int32) + (ib < n_blk - 1).astype(jnp.int32)
-    along = 1 + (iy > 0).astype(jnp.int32) + (iy < n_sub - 1).astype(jnp.int32)
-    pl.semaphore_wait(barrier, across * along - 1)
-
-    def fine_copies(src, dst, sem, width):
-        copies = []
-        for k, (dx, dy) in enumerate(DIRS):
-            count = width - abs(dy)
-            block = src.at[send_range(dx, 3, 16, count), send_range(dy, 0, 32, 4)]
-            target = dst.at[planes_to(dx, 3, 16, count), rows_to(dy, 32, 4)]
-            copies.append(remote(block, target, sem, k, dx, dy))
-        return copies
-
-    d_copies = fine_copies(d, d, d_sem, 3)
     ps_copies = []
     for k, (dx, dy) in enumerate(DIRS):
         block = ps.at[:, send_range(dx, 3, 16, 2), send_range(dy, 0, 32, 4)]
@@ -250,7 +254,7 @@
             block = sx.at[0 if dx < 0 else 1]
         target = ps.at[:, planes_to(dx, 3, 16, 2), rows_to(dy, 32, 4)]
         ps_copies.append(remote(block, target, ps_sem, k, dx, dy))
-    for copy in d_copies + ps_copies:
+    for copy in ps_copies:
         copy.start()
 
     for copy in d_copies:

time: 32.1 us -> 32 us (level)
  no operation moved by 1% of the time
where the time goes in v8:
time: 32 us; the launch traced here: 31.9 us
  Pallas kernels  31.2 us (98%)
  local copies, waits for them, and re-layouts  0.71 us (2%)
    pallas_call x1, Pallas kernels, on_device(): pl.pallas_call(functools.partial(kernel, sizes), out_shape=jax.ShapeDtype...  31.2 us
    unnamed x1, local copies, waits for them, and re-layouts  0.71 us

profile of v8, /device:TPU:1, one launch (start us, length us, event | category | flops | bytes accessed | tf_op | source)
XLA Modules:
  0.0 31.9 jit_solution(2533433193877853197)
XLA Ops:
  0.0 31.2 %shard_map.37 = f32[16,32,128]{2,1,0:T(8,128)S(1)} custom-call(f32[16,32,128]{2,1,0:T(8,128)} %p_hbm.1, f32[16,32,128]{2,1,0:T(8,128)} %s_hbm.1, f32[16,32,128]{2,1,0:T(8,128)} %d_hbm.1), custom_call_target="tpu_custom_call" | custom-call | tf_op jit(solution)/shard_map/pallas_call | solution.py:544
  31.2 0.7 %copy.5 = f32[16,32,128]{2,1,0:T(8,128)} copy(f32[16,32,128]{2,1,0:T(8,128)S(1)} %shard_map.37) | data formatting | bytes 524288

commit v9 on v4

--- a/solution.py
+++ b/solution.py
@@ -407,7 +407,7 @@
         for k, (dx, dy) in enumerate(DIRS)
     ]
     f_copies = fine_copies(v2, fh, f_sem, 2)
-    for copy in b1_copies + c2_copies:
+    for copy in b1_copies + c2_copies + f_copies:
         copy.start()
 
     for copy in l1_copies:
@@ -434,7 +434,7 @@
         )
         for k, (dx, dy) in enumerate(FAR)
     ]
-    for copy in b2_copies + f_copies:
+    for copy in b2_copies:
         copy.start()
     for copy in c2_copies:
         copy.wait_recv()

time: 31.9 us -> 31.9 us (level)
  no operation moved by 1% of the time
where the time goes in v9:
time: 31.9 us; the launch traced here: 31.7 us
  Pallas kernels  31 us (97%)
  local copies, waits for them, and re-layouts  0.71 us (2%)
    pallas_call x1, Pallas kernels, on_device(): pl.pallas_call(functools.partial(kernel, sizes), out_shape=jax.ShapeDtype...  31 us
    unnamed x1, local copies, waits for them, and re-layouts  0.71 us

profile of v9, /device:TPU:1, one launch (start us, length us, event | category | flops | bytes accessed | tf_op | source)
XLA Modules:
  0.0 31.7 jit_solution(12113381701363490110)
XLA Ops:
  0.0 31.0 %shard_map.37 = f32[16,32,128]{2,1,0:T(8,128)S(1)} custom-call(f32[16,32,128]{2,1,0:T(8,128)} %p_hbm.1, f32[16,32,128]{2,1,0:T(8,128)} %s_hbm.1, f32[16,32,128]{2,1,0:T(8,128)} %d_hbm.1), custom_call_target="tpu_custom_call" | custom-call | tf_op jit(solution)/shard_map/pallas_call | solution.py:534
  31.0 0.7 %copy.5 = f32[16,32,128]{2,1,0:T(8,128)} copy(f32[16,32,128]{2,1,0:T(8,128)S(1)} %shard_map.37) | data formatting | bytes 524288
